TPU v7x, 768 devices: a whole 4x8x12 slice. The times are simulated.
768 devices in a mesh: dp: 32 (over y_lo, x, core), expert: 24 (over y_hi, z).
Axes of the slice: x: 4, y: 8 (y_hi: 2, y_lo: 4; y = y_hi * 4 + y_lo), z: 12, core: 2. Of those that a mesh axis runs over, the one named last changes fastest.
Arguments:
- frames: bfloat16 [4096, 1536], P('dp', 'expert'), may hold values from -6 to 6
- cotangent: bfloat16 [4096, 1536], P('dp', 'expert'), may hold values from -6 to 6
- routes: int32 [4096, 2], P('dp'), may hold values from 0 to 23, all different within a row; in each aligned block of 128 rows (0 to 127, 128 to 255, ...) at most 16 rows name the same one
- route_gates: float32 [4096, 2], P('dp'), may hold values from 0.25 to 1
- norm_gain: float32 [1536], replicated, may hold values from 0.1 to 1.9
- norm_bias: float32 [1536], replicated, may hold values from -3 to 3
- expert_in: bfloat16 [24, 1536, 6144], P('expert', None, 'dp'), may hold values from -0.15625 to 0.15625
- expert_out: bfloat16 [24, 6144, 1536], P('expert', 'dp'), may hold values from -0.078125 to 0.078125
Outputs:
- output: bfloat16 [4096, 1536], P('dp', 'expert')
- frame_grads: bfloat16 [4096, 1536], P('dp', 'expert')
- grad_in: float32 [24, 1536, 6144], P('expert', None, 'dp')
- grad_out: float32 [24, 6144, 1536], P('expert', 'dp')
Inputs may be any that keep to these rules, and one draw needn't show every extreme that they name: `routes`: each frame names two different experts. Within each aligned block of 128 frames no expert is named more than 16 times, a bound that some block reaches.
All inputs are finite; a program needn't handle non-finite values.
Results may differ from a plain program's by a relative error of at most 0.015.
Values may be sent and summed in bfloat16 or wider, within the bound.
No kernel may reach another device: no remote copies, remote signals or barrier semaphores. Data moves between devices by JAX's collectives and lax.ppermute only.
A program may use at most 64 MiB of HBM per device.

v0:
```python
import jax
import jax.numpy as jnp
from jax import lax
from jax.sharding import PartitionSpec as P

epsilon = 1e-05


def normalize(rows, norm_gain, norm_bias):
    values = rows.astype(jnp.float32)
    row_mean = jnp.mean(values, axis=-1, keepdims=True)
    centered = values - row_mean
    row_var = jnp.mean(centered * centered, axis=-1, keepdims=True)
    scaled = lax.rsqrt(row_var + epsilon)
    unit = centered * scaled
    normed = (unit * norm_gain + norm_bias).astype(jnp.bfloat16)
    return (normed, unit, scaled)


def body(frames, cotangent, routes, route_gates, norm_gain, norm_bias, expert_in, expert_out):
    expert_count = lax.axis_size("expert")
    tok_rows = frames.shape[0]
    capacity = 3 * tok_rows // expert_count
    width = norm_gain.shape[0]
    flat_routes = routes.reshape(-1)
    onehot = (flat_routes[:, None] == jnp.arange(expert_count, dtype=jnp.int32)[None, :]).astype(
        jnp.int32
    )
    earlier = jnp.cumsum(onehot, axis=0) - onehot
    slots = jnp.sum(earlier * onehot, axis=1)
    target = flat_routes * capacity + slots
    placing = target[None, :] == jnp.arange(expert_count * capacity, dtype=jnp.int32)[:, None]
    scales = 0.5 * route_gates.reshape(-1)
    weighted = placing.astype(jnp.float32) * scales[None, :]
    frame_pairs = jnp.repeat(frames, 2, axis=0)
    grad_pairs = jnp.repeat(cotangent, 2, axis=0).astype(jnp.float32)
    sent_rows = jnp.dot(
        placing.astype(jnp.bfloat16), frame_pairs, preferred_element_type=jnp.float32
    ).astype(jnp.bfloat16)
    sent_grads = jnp.dot(weighted, grad_pairs, precision=lax.Precision.HIGHEST).astype(jnp.bfloat16)
    sent_rows = sent_rows.reshape(expert_count, capacity, -1)
    sent_grads = sent_grads.reshape(expert_count, capacity, -1)
    own_rows, own_grads = (
        lax.all_to_all(sent_rows, "expert", split_axis=0, concat_axis=2, tiled=True),
        lax.all_to_all(sent_grads, "expert", split_axis=0, concat_axis=2, tiled=True),
    )
    own_rows = own_rows.reshape(capacity, width)
    own_grads = own_grads.reshape(capacity, width)
    weight_in = expert_in[0]
    weight_out = expert_out[0]
    own_normed, own_unit, own_scaled = normalize(own_rows, norm_gain, norm_bias)
    all_rows, all_grads = (
        lax.all_gather(own_rows, "dp", axis=0, tiled=True),
        lax.all_gather(own_grads, "dp", axis=0, tiled=True),
    )
    all_normed = normalize(all_rows, norm_gain, norm_bias)[0]
    inner = jnp.dot(all_normed, weight_in, preferred_element_type=jnp.float32)
    hidden = jax.nn.silu(inner).astype(jnp.bfloat16)
    back_hidden = jnp.dot(all_grads, weight_out.T, preferred_element_type=jnp.float32)
    sigm = jax.nn.sigmoid(inner)
    back_inner = (back_hidden * sigm * (1.0 + inner * (1.0 - sigm))).astype(jnp.bfloat16)
    grad_out = jnp.dot(hidden.T, all_grads, preferred_element_type=jnp.float32)
    grad_in = jnp.dot(all_normed.T, back_inner, preferred_element_type=jnp.float32)
    forward_part = jnp.dot(hidden, weight_out, preferred_element_type=jnp.float32)
    backward_part = jnp.dot(back_inner, weight_in.T, preferred_element_type=jnp.float32)
    part = jnp.concatenate([forward_part, backward_part], axis=1).astype(jnp.bfloat16)
    joined = lax.psum_scatter(
        lax.optimization_barrier(part).astype(jnp.float32).astype(jnp.bfloat16),
        "dp",
        scatter_dimension=0,
        tiled=True,
    ).astype(jnp.float32)
    result_sum = joined[:, :width]
    back_sum = joined[:, width:]
    back_unit = back_sum * norm_gain
    first = jnp.mean(back_unit, axis=-1, keepdims=True)
    second = jnp.mean(back_unit * own_unit, axis=-1, keepdims=True)
    back_rows = ((back_unit - first - own_unit * second) * own_scaled).astype(jnp.bfloat16)
    result_rows = result_sum.astype(jnp.bfloat16)
    came_results, came_backs = (
        lax.all_to_all(
            result_rows.reshape(1, capacity, width),
            "expert",
            split_axis=2,
            concat_axis=0,
            tiled=True,
        ),
        lax.all_to_all(
            back_rows.reshape(1, capacity, width), "expert", split_axis=2, concat_axis=0, tiled=True
        ),
    )
    came_results = came_results.reshape(expert_count * capacity, -1).astype(jnp.float32)
    came_backs = came_backs.reshape(expert_count * capacity, -1).astype(jnp.float32)
    taken = jnp.dot(weighted.T, came_results, precision=lax.Precision.HIGHEST)
    output = (frames.astype(jnp.float32) + jnp.sum(taken.reshape(tok_rows, 2, -1), axis=1)).astype(
        jnp.bfloat16
    )
    taken_back = jnp.dot(placing.astype(jnp.float32).T, came_backs, precision=lax.Precision.HIGHEST)
    frame_grads = (
        cotangent.astype(jnp.float32) + jnp.sum(taken_back.reshape(tok_rows, 2, -1), axis=1)
    ).astype(jnp.bfloat16)
    return (output, frame_grads, grad_in[None], grad_out[None])


def solution(mesh):
    placed = (
        P("dp", "expert"),
        P("dp", "expert"),
        P("dp", None),
        P("dp", None),
        P(),
        P(),
        P("expert", None, "dp"),
        P("expert", "dp", None),
    )
    return jax.shard_map(
        body,
        mesh=mesh,
        in_specs=placed,
        out_specs=(
            P("dp", "expert"),
            P("dp", "expert"),
            P("expert", None, "dp"),
            P("expert", "dp", None),
        ),
        check_vma=False,
    )
```

profile of v0, /device:TPU:64, one launch (start us, length us, event | category | flops | bytes accessed | tf_op | source)
XLA Modules:
  0.0 399.2 jit_solution(5250123985857177356)
XLA Ops:
  7.2 0.8 copy.74
  8.1 0.1 reshape.159
  8.2 0.1 eq.67
  8.4 0.8 copy.78
  9.2 0.6 reduce-window.6
  9.8 0.2 slice_reduce_fusion
  10.2 0.2 convolution_convert_fusion.2
  10.4 0.1 copy.79
  10.5 0.1 reshape.176
  10.7 33.3 %all_to_all.60 = bf16[24,2,512]{2,1,0:T(2,128)(2,1)S(1)} all-to-all(bf16[24,2,512]{2,1,0:T(2,128)(2,1)S(1)} %reshape.176), channel_id=1, replica_groups=mesh['dp'=32,'expert'=24] {'expert'}, dimensions={0} | all-to-all | bytes 98304 | tf_op jit(solution)/shard_map/all_to_all | solution.py:44
  44.0 0.1 reshape.177
  44.2 0.7 reshape.163
  45.0 0.1 copy.82
  45.1 0.1 copy.81
  45.2 0.1 mul.131
  45.4 0.4 convolution_convert_fusion.3
  45.8 0.1 copy.83
  45.9 0.1 reshape.174
  46.1 17.9 %all_to_all.61 = bf16[24,2,512]{2,1,0:T(2,128)(2,1)S(1)} all-to-all(bf16[24,2,512]{2,1,0:T(2,128)(2,1)S(1)} %reshape.174), channel_id=1, replica_groups=mesh['dp'=32,'expert'=24] {'expert'}, dimensions={0} | all-to-all | bytes 98304 | tf_op jit(solution)/shard_map/all_to_all | solution.py:45
  64.0 0.1 reshape.175
  64.1 0.8 reshape.166
  65.0 36.1 %all-gather.3.cloned.1.call-done = bf16[512,1536]{1,0:T(8,128)(2,1)} async-done(((bf16[16,1536]{1,0:T(8,128)(2,1)}), bf16[512,1536]{1,0:T(8,128)(2,1)}) %all-gather.3.cloned.1.call-update) | async-done | bytes 1572880 | tf_op jit(solution)/shard_map/all_gather | solution.py:53
  101.0 1.8 convert_reduce_fusion
  102.9 0.5 fusion.2
  103.5 0.7 fusion.5
  104.2 0.4 copy-done.2
  104.6 0.7 fusion.11
  105.2 1.8 convolution_convert_fusion.1
  107.0 61.2 %all-gather.5.cloned.1.call-done = bf16[512,1536]{1,0:T(8,128)(2,1)} async-done(((bf16[16,1536]{1,0:T(8,128)(2,1)}), bf16[512,1536]{1,0:T(8,128)(2,1)}) %all-gather.5.cloned.1.call-update) | async-done | bytes 1572880 | tf_op jit(solution)/shard_map/all_gather | solution.py:54
  168.3 2.1 fusion.7
  170.4 0.6 convolution_convert_fusion
  171.0 0.8 copy-done.3
  171.8 2.0 pad_maximum_fusion
  173.8 0.1 reduce_sum.84
  174.0 0.5 copy-done.10
  174.5 0.1 convert_reduce_fusion.1
  174.6 0.2 fusion.19
  174.9 1.5 convolution_bitcast_fusion
  176.4 1.5 convolution_bitcast_fusion.1
  177.9 149.4 %reduce-scatter.2.cloned.1.call-done = bf16[16,3072]{1,0:T(8,128)(2,1)} async-done(((bf16[512,3072]{1,0:T(8,128)(2,1)}), bf16[16,3072]{1,0:T(8,128)(2,1)}) %reduce-scatter.2.cloned.1.call-update) | async-done | bytes 98320 | tf_op jit(solution)/shard_map/reduce_scatter | solution.py:67
  327.3 0.9 slice_bitcast_fusion
  328.1 0.5 copy.85
  328.7 0.5 broadcast.167
  329.2 8.8 %reduce.4 = bf16[1536,16]{1,0:T(8,128)(2,1)S(1)} reduce(bf16[1536,1,16]{2,1,0:T(2,128)(2,1)S(1)} %bitcast.81, bf16[]{:T(256)} %broadcast.167), dimensions={1}, to_apply=%bitcast.66.reduce_sub_computation | reduce | bytes 98306
  338.0 1.1 reshape.178
  339.1 12.8 %all-to-all-start.2 = ((bf16[24,2,512]{2,1,0:T(2,128)(2,1)}), bf16[24,2,512]{2,1,0:T(2,128)(2,1)S(1)}, u32[]{:S(2)}, u32[]{:S(2)}) async-start(bf16[24,2,512]{2,1,0:T(2,128)(2,1)} %reshape.178), calls=%async_computation.3 | async-start | bytes 98304 | tf_op jit(solution)/shard_map/all_to_all | solution.py:81
  351.9 0.2 fusion.28
  352.1 0.1 fusion.29
  352.2 0.6 copy.89
  352.8 8.8 %reduce.5 = bf16[1536,16]{1,0:T(8,128)(2,1)S(1)} reduce(bf16[1536,1,16]{2,1,0:T(2,128)(2,1)S(1)} %bitcast.82, bf16[]{:T(256)} %broadcast.167), dimensions={1}, to_apply=%bitcast.68.reduce_sub_computation | reduce | bytes 98306
  361.6 1.1 reshape.180
  362.6 2.6 all-to-all-done.2
  365.3 11.9 %all-to-all-start.3 = ((bf16[24,2,512]{2,1,0:T(2,128)(2,1)}), bf16[24,2,512]{2,1,0:T(2,128)(2,1)S(1)}, u32[]{:S(2)}, u32[]{:S(2)}) async-start(bf16[24,2,512]{2,1,0:T(2,128)(2,1)} %reshape.180), calls=%async_computation.4 | async-start | bytes 98304 | tf_op jit(solution)/shard_map/all_to_all | solution.py:88
  377.1 0.7 reshape.179
  377.9 0.4 copy.86
  378.2 0.1 all_to_all.51
  378.4 0.4 convolution_reduce_fusion.1
  378.8 0.6 add_convert_fusion.1
  379.5 11.1 %all-to-all-done.3 = bf16[24,2,512]{2,1,0:T(2,128)(2,1)S(1)} async-done(((bf16[24,2,512]{2,1,0:T(2,128)(2,1)}), bf16[24,2,512]{2,1,0:T(2,128)(2,1)S(1)}, u32[]{:S(2)}, u32[]{:S(2)}) %all-to-all-start.3) | async-done | bytes 49184 | tf_op jit(solution)/shard_map/all_to_all | solution.py:88
  390.6 0.7 reshape.181
  391.3 0.4 copy.90
  391.6 0.1 all_to_all.54
  391.8 0.3 convolution_reduce_fusion
  392.1 0.6 add_convert_fusion
  (48 shorter events, 0.7 us)
Async XLA Ops:
  7.2 98.1 %copy-start = (bf16[1,192,1536]{2,1,0:T(8,128)(2,1)S(1)}, bf16[1,192,1536]{2,1,0:T(8,128)(2,1)}, u32[]{:S(2)}) copy-start(bf16[1,192,1536]{2,1,0:T(8,128)(2,1)} %param.15) | copy-start | bytes 1769476
  7.2 37.8 %copy-start.8 = (bf16[128,64]{0,1:T(8,128)(2,1)S(1)}, bf16[128,64]{0,1:T(8,128)(2,1)}, u32[]{:S(2)}) copy-start(bf16[128,64]{0,1:T(8,128)(2,1)} %param.9) | copy-start | bytes 49156
  7.2 37.9 %copy-start.11 = (f32[128,2]{0,1:T(2,128)S(1)}, f32[128,2]{0,1:T(2,128)}, u32[]{:S(2)}) copy-start(f32[128,2]{0,1:T(2,128)} %param.11) | copy-start | bytes 3076
  7.2 93.8 %all-gather.3.cloned.1.call-start = ((), (), s32[]{:S(2)}) async-start(), calls=%async_computation.5 | async-start | bytes 1622016 | tf_op jit(solution)/shard_map/all_gather | solution.py:53
  44.9 123.3 %all-gather.5.cloned.1.call-start = ((), (), s32[]{:S(2)}) async-start(), calls=%async_computation.6 | async-start | bytes 1622016 | tf_op jit(solution)/shard_map/all_gather | solution.py:54
  64.9 38.6 %copy-start.6 = (f32[1536]{0:T(1024)S(1)}, f32[1536]{0:T(1024)}, u32[]{:S(2)}) copy-start(f32[1536]{0:T(1024)} %param.12) | copy-start | bytes 18436
  64.9 38.6 %copy-start.9 = (f32[1536]{0:T(1024)S(1)}, f32[1536]{0:T(1024)}, u32[]{:S(2)}) copy-start(f32[1536]{0:T(1024)} %param.13) | copy-start | bytes 18436
  64.9 262.3 %reduce-scatter.2.cloned.1.call-start = ((), (), s32[]{:S(2)}) async-start(), calls=%async_computation.7 | async-start | bytes 3244032 | tf_op jit(solution)/shard_map/reduce_scatter | solution.py:67
  101.0 1.9 copy-start.1
  103.5 1.1 copy-start.2
  170.4 1.4 copy-start.3
  173.8 0.7 copy-start.10
  174.5 1.9 copy-start.12
  177.9 174.0 %copy-start.4 = (bf16[16,1536]{1,0:T(8,128)(2,1)S(1)}, bf16[16,1536]{1,0:T(8,128)(2,1)}, u32[]{:S(2)}) copy-start(bf16[16,1536]{1,0:T(8,128)(2,1)} %reshape.163) | copy-start | bytes 147460
  327.3 24.6 %copy-start.5 = (bf16[16,3072]{1,0:T(8,128)(2,1)S(1)}, bf16[16,3072]{1,0:T(8,128)(2,1)}, u32[]{:S(2)}) copy-start(bf16[16,3072]{1,0:T(8,128)(2,1)} %reduce-scatter.2.cloned.1.call-done) | copy-start | bytes 294916
  339.1 26.2 %all-to-all-start.2 = ((bf16[24,2,512]{2,1,0:T(2,128)(2,1)}), bf16[24,2,512]{2,1,0:T(2,128)(2,1)S(1)}, u32[]{:S(2)}, u32[]{:S(2)}) async-start(bf16[24,2,512]{2,1,0:T(2,128)(2,1)} %reshape.178), calls=%async_computation.3 | async-start | bytes 98304 | tf_op jit(solution)/shard_map/all_to_all | solution.py:81
  361.6 17.3 %copy-start.7 = (bf16[128,64]{0,1:T(8,128)(2,1)S(1)}, bf16[128,64]{0,1:T(8,128)(2,1)}, u32[]{:S(2)}) copy-start(bf16[128,64]{0,1:T(8,128)(2,1)} %param.8) | copy-start | bytes 49156
  365.3 25.3 %all-to-all-start.3 = ((bf16[24,2,512]{2,1,0:T(2,128)(2,1)}), bf16[24,2,512]{2,1,0:T(2,128)(2,1)S(1)}, u32[]{:S(2)}, u32[]{:S(2)}) async-start(bf16[24,2,512]{2,1,0:T(2,128)(2,1)} %reshape.180), calls=%async_computation.4 | async-start | bytes 98304 | tf_op jit(solution)/shard_map/all_to_all | solution.py:88
Sparse Core Ops, SparseCore 0:
  45.0 55.9 all-gather.2
  104.0 64.1 all-gather.4
  174.0 153.2 reduce-scatter.1
where the time goes:
time: 400 us; the launch traced here: 399 us
  waiting for transfers between devices  260 us (65%)
  blocking collectives  51.2 us (13%)
  other arithmetic  25.3 us (6%)
  starting transfers between devices  24.8 us (6%)
  between operations  14.1 us (4%)
  local copies, waits for them, and re-layouts  13.9 us (3%)
  matrix products  9.45 us (2%)
    reduce_scatter x1, waiting for transfers between devices, body(): lax.psum_scatter(lax.optimization_barrier(part).astype(jnp.float32).astyp...  149 us
    all_gather x1, waiting for transfers between devices, body(): lax.all_gather(own_grads, 'dp', axis=0, tiled=True)  61.2 us
    all_gather x1, waiting for transfers between devices, body(): lax.all_gather(own_rows, 'dp', axis=0, tiled=True)  36.1 us
    all_to_all x1, blocking collectives, body(): lax.all_to_all(sent_rows, 'expert', split_axis=0, concat_axis=2, tiled=True)  33.3 us
    all_to_all x1, blocking collectives, body(): lax.all_to_all(sent_grads, 'expert', split_axis=0, concat_axis=2, tiled=T...  17.9 us
    unnamed x2, other arithmetic  17.6 us
    all_to_all x1, starting transfers between devices, body(): lax.all_to_all(result_rows.reshape(1, capacity, width), 'expert', split_a...  12.8 us
    all_to_all x1, starting transfers between devices, body(): lax.all_to_all(back_rows.reshape(1, capacity, width), 'expert', split_axi...  11.9 us
  transfers between devices with their start and end apart: 5, of which 5 were waited for; matrix products, arithmetic and copies ran while one was open for 6% of the time, Pallas kernels for 0%

commit v1 on v0

v1 whole, which is shorter than its diff:
```python
import jax
import jax.numpy as jnp
from jax import lax
from jax.experimental import pallas as pl
from jax.experimental.pallas import tpu as pltpu
from jax.sharding import Mesh
from jax.sharding import PartitionSpec as P

epsilon = 1e-05
LANES = 128
HALF = 64
Y_LO, X, CORE, Y_HI, Z = 4, 4, 2, 2, 12
EXPERTS = Y_HI * Z
CAP = 16
SLOTS = EXPERTS * CAP
ROWS = Y_LO * CAP
DP_AXES = ("yl", "x", "core")
EXPERT_AXES = ("yh", "z")
F32 = jnp.float32
BF16 = jnp.bfloat16


def call(kernel, out_shapes, flops=0, bytes_accessed=0):
    return pl.pallas_call(
        kernel,
        out_shape=out_shapes,
        compiler_params=pltpu.CompilerParams(vmem_limit_bytes=40 * 1024 * 1024),
        cost_estimate=pl.CostEstimate(
            flops=flops, bytes_accessed=bytes_accessed, transcendentals=0
        ),
    )


def dot(a, b, ca, cb):
    return lax.dot_general(a, b, (((ca,), (cb,)), ((), ())), preferred_element_type=F32)


def places(routes):
    tokens = routes.shape[1]
    first, second = routes[0:1], routes[1:2]
    experts = lax.broadcasted_iota(jnp.int32, (EXPERTS, tokens), 0)
    names = (experts == first, experts == second)
    either = (names[0] | names[1]).astype(F32)
    before = lax.broadcasted_iota(jnp.int32, (tokens, tokens), 0) < lax.broadcasted_iota(
        jnp.int32, (tokens, tokens), 1
    )
    earlier = dot(either.astype(BF16), before.astype(F32).astype(BF16), 1, 0)
    rows = lax.broadcasted_iota(jnp.int32, (SLOTS, tokens), 0)
    masks = []
    for name, expert in zip(names, (first, second)):
        slot = jnp.sum(jnp.where(name, earlier, 0.0), axis=0, keepdims=True)
        masks.append(rows == expert * CAP + slot.astype(jnp.int32))
    return masks


def route_kernel(routes_ref, gates_ref, frames_ref, cotangent_ref, out_ref):
    mask0, mask1 = places(routes_ref[...])
    gates = 0.5 * gates_ref[...]
    scale = jnp.sum(
        jnp.where(mask0, gates[0:1], 0.0) + jnp.where(mask1, gates[1:2], 0.0),
        axis=1,
        keepdims=True,
    )
    chosen = (mask0 | mask1).astype(F32).astype(BF16)
    both = jnp.concatenate([frames_ref[...], cotangent_ref[...]], axis=0)
    picked = dot(chosen, both, 1, 1)
    lane = lax.broadcasted_iota(jnp.int32, picked.shape, 1)
    sent = jnp.where(lane < HALF, picked, picked * scale).astype(BF16)
    sent = sent.reshape(EXPERTS, CAP, LANES)
    for y in range(Y_LO):
        out_ref[y] = sent


def swap_halves(a):
    return pltpu.roll(a, HALF, 1)


def normal(rows):
    mean = jnp.mean(rows, axis=-1, keepdims=True)
    centered = rows - mean
    var = jnp.mean(centered * centered, axis=-1, keepdims=True)
    scaled = lax.rsqrt(var + epsilon)
    return centered * scaled, scaled


def normalize_kernel(came_ref, gain_ref, bias_ref, sent_ref, rows_ref, values_ref):
    lane = lax.broadcasted_iota(jnp.int32, (ROWS, LANES), 1)
    for p in range(EXPERTS // 2):
        a = came_ref[:, 2 * p].astype(F32).reshape(ROWS, LANES)
        b = came_ref[:, 2 * p + 1].astype(F32).reshape(ROWS, LANES)
        cols = slice(p * LANES, (p + 1) * LANES)
        values_ref[:, cols] = jnp.where(lane < HALF, a, swap_halves(b))
        sent_ref[ROWS:, cols] = jnp.where(lane < HALF, swap_halves(a), b).astype(BF16)
    values = values_ref[...]
    rows_ref[...] = values.astype(BF16)
    unit, _ = normal(values)
    sent_ref[:ROWS] = (unit * gain_ref[...] + bias_ref[...]).astype(BF16)


def expert_kernel(
    x0, x1, x2, x3, in_own, in_sib, out_own, out_sib, p0, p1, p2, p3, hid_ref, back_ref
):
    width = x0.shape[1]
    normed = jnp.concatenate([x[:ROWS] for x in (x0, x1, x2, x3)], axis=0)
    grads = jnp.concatenate([x[ROWS:] for x in (x0, x1, x2, x3)], axis=0)
    weight_in = jnp.concatenate([in_own[...], in_sib[...]], axis=0)
    weight_out = jnp.concatenate([out_own[...], out_sib[...]], axis=0)
    inner = dot(normed, weight_in, 1, 1)
    back_hidden = dot(grads, weight_out, 1, 1)
    sigm = jax.nn.sigmoid(inner)
    hidden = (inner * sigm).astype(BF16)
    back_inner = (back_hidden * sigm * (1.0 + inner * (1.0 - sigm))).astype(BF16)
    hid_ref[...] = hidden
    back_ref[...] = back_inner
    for i, p in enumerate((p0, p1, p2, p3)):
        rows = slice(i * ROWS, (i + 1) * ROWS)
        p[:, :width] = dot(hidden[rows], weight_out, 1, 0).astype(p.dtype)
        p[:, width:] = dot(back_inner[rows], weight_in, 1, 0).astype(p.dtype)


def grads_kernel(x0, x1, x2, x3, hid_ref, back_ref, in_ref, out_ref, sib_ref):
    normed = jnp.concatenate([x[:ROWS] for x in (x0, x1, x2, x3)], axis=0)
    grads = jnp.concatenate([x[ROWS:] for x in (x0, x1, x2, x3)], axis=0)
    half = in_ref.shape[0]
    grad_in = dot(back_ref[...], normed, 0, 0)
    in_ref[...] = grad_in[:half]
    sib_ref[:half] = grad_in[half:].astype(BF16)
    grad_out = dot(hid_ref[...], grads, 0, 0)
    out_ref[...] = grad_out[:half]
    sib_ref[half:] = grad_out[half:].astype(BF16)


def back_kernel(p0, p1, p2, p3, rows_ref, gain_ref, out_ref):
    width = rows_ref.shape[1]

    def total(cols):
        return (
            p0[:, cols].astype(F32)
            + p1[:, cols].astype(F32)
            + p2[:, cols].astype(F32)
            + p3[:, cols].astype(F32)
        )

    unit, scaled = normal(rows_ref[...].astype(F32))
    back_unit = total(slice(width, 2 * width)) * gain_ref[...]
    first = jnp.mean(back_unit, axis=-1, keepdims=True)
    second = jnp.mean(back_unit * unit, axis=-1, keepdims=True)
    back = (back_unit - first - unit * second) * scaled
    lane = lax.broadcasted_iota(jnp.int32, (ROWS, LANES), 1)
    for p in range(EXPERTS // 2):
        cols = slice(p * LANES, (p + 1) * LANES)
        a, b = total(cols), back[:, cols]
        low = jnp.where(lane < HALF, a, swap_halves(b))
        high = jnp.where(lane < HALF, swap_halves(a), b)
        out_ref[:, 2 * p] = low.astype(BF16).reshape(Y_LO, CAP, LANES)
        out_ref[:, 2 * p + 1] = high.astype(BF16).reshape(Y_LO, CAP, LANES)


def combine_kernel(came_ref, routes_ref, gates_ref, frames_ref, cotangent_ref, out_ref, fg_ref):
    total = came_ref[0].astype(F32)
    for y in range(1, Y_LO):
        total = total + came_ref[y].astype(F32)
    came = total.astype(BF16).reshape(SLOTS, LANES)
    gates = 0.5 * gates_ref[...]
    taken = [dot(came, mask.astype(F32).astype(BF16), 0, 0) for mask in places(routes_ref[...])]
    results = taken[0][:HALF] * gates[0:1] + taken[1][:HALF] * gates[1:2]
    backs = taken[0][HALF:] + taken[1][HALF:]
    out_ref[...] = (frames_ref[...].astype(F32) + results).astype(BF16)
    fg_ref[...] = (cotangent_ref[...].astype(F32) + backs).astype(BF16)


def ring(size, step):
    return [(i, (i + step) % size) for i in range(size)]


def body(frames, cotangent, routes, route_gates, norm_gain, norm_bias, expert_in, expert_out):
    width = norm_gain.shape[0]
    units = expert_out.shape[1]
    frames_t, cotangent_t = frames.T, cotangent.T
    routes_t, gates_t = routes.T, route_gates.T
    gain, bias = norm_gain[None], norm_bias[None]
    in_own, out_own = expert_in[0].T, expert_out[0]
    shape = jax.ShapeDtypeStruct
    blocks = shape((Y_LO, EXPERTS, CAP, LANES), BF16)

    def exchange(a):
        a = a.reshape(Y_LO * EXPERTS, CAP, LANES)
        a = lax.all_to_all(a, ("yl",) + EXPERT_AXES, split_axis=0, concat_axis=0, tiled=True)
        return a.reshape(Y_LO, EXPERTS, CAP, LANES)

    in_sib = lax.ppermute(in_own, "core", ring(CORE, 1))
    out_sib = lax.ppermute(out_own, "core", ring(CORE, 1))
    came = exchange(call(route_kernel, blocks)(routes_t, gates_t, frames_t, cotangent_t))
    mine, rows = pl.pallas_call(
        normalize_kernel,
        out_shape=(shape((2 * ROWS, width), BF16), shape((ROWS, width), BF16)),
        scratch_shapes=[pltpu.VMEM((ROWS, width), F32)],
        compiler_params=pltpu.CompilerParams(vmem_limit_bytes=40 * 1024 * 1024),
    )(came, gain, bias)
    all_x = [mine] + [lax.ppermute(mine, "x", ring(X, step)) for step in (1, 3, 2)]
    part = shape((ROWS, 2 * width), BF16)
    kept = shape((X * ROWS, CORE * units), BF16)
    p0, p1, p3, p2, hidden, back_inner = call(
        expert_kernel, (shape((ROWS, 2 * width), F32), part, part, part, kept, kept)
    )(*all_x, in_own, in_sib, out_own, out_sib)
    r1 = lax.ppermute(p1, "x", ring(X, 3))
    r3 = lax.ppermute(p3, "x", ring(X, 1))
    r2 = lax.ppermute(p2, "x", ring(X, 2))
    grad_in, grad_out, for_sib = call(
        grads_kernel,
        (
            shape((units, width), F32),
            shape((units, width), F32),
            shape((2 * units, width), BF16),
        ),
        flops=4 * X * ROWS * CORE * units * width,
        bytes_accessed=8 * units * width * 4,
    )(*all_x, hidden, back_inner)
    from_sib = lax.ppermute(for_sib, "core", ring(CORE, 1)).astype(F32)
    grad_in = grad_in + from_sib[:units]
    grad_out = grad_out + from_sib[units:]
    backs = exchange(call(back_kernel, blocks)(p0, r1, r2, r3, rows, gain))
    token = shape(frames_t.shape, BF16)
    output, frame_grads = call(combine_kernel, (token, token))(
        backs, routes_t, gates_t, frames_t, cotangent_t
    )
    return (output.T, frame_grads.T, grad_in.T[None], grad_out[None])


def solution(mesh):
    fine = Mesh(mesh.devices.reshape(Y_LO, X, CORE, Y_HI, Z), DP_AXES + EXPERT_AXES)
    tokens = P(DP_AXES, EXPERT_AXES)
    weights_in = P(EXPERT_AXES, None, DP_AXES)
    weights_out = P(EXPERT_AXES, DP_AXES, None)
    return jax.shard_map(
        body,
        mesh=fine,
        in_specs=(
            tokens,
            tokens,
            P(DP_AXES, None),
            P(DP_AXES, None),
            P(),
            P(),
            weights_in,
            weights_out,
        ),
        out_specs=(tokens, tokens, weights_in, weights_out),
        check_vma=False,
    )
```

time: 400 us -> 138 us (0.34)
  the two profiles are of different devices: /device:TPU:64 before, /device:TPU:8 now
where the time goes in v1:
time: 138 us; the launch traced here: 137 us
  waiting for transfers between devices  64.9 us (47%)
  starting transfers between devices  57.1 us (41%)
  Pallas kernels  8.27 us (6%)
  other arithmetic  3.34 us (2%)
  local copies, waits for them, and re-layouts  2.93 us (2%)
    all_to_all x2, waiting for transfers between devices, exchange(): lax.all_to_all(a, ('yl',) + EXPERT_AXES, split_axis=0, concat_axis=0, til...  37.8 us
    all_to_all x2, starting transfers between devices, exchange(): lax.all_to_all(a, ('yl',) + EXPERT_AXES, split_axis=0, concat_axis=0, til...  30.6 us
    ppermute x1, waiting for transfers between devices, body(): r1 = lax.ppermute(p1, 'x', ring(X, 3))  12 us
    ppermute x3, starting transfers between devices, body(): lax.ppermute(mine, 'x', ring(X, step))  10.8 us
    ppermute x3, waiting for transfers between devices, body(): lax.ppermute(mine, 'x', ring(X, step))  9.55 us
    ppermute x1, waiting for transfers between devices, body(): r3 = lax.ppermute(p3, 'x', ring(X, 1))  5.58 us
    ppermute x1, starting transfers between devices, body(): r1 = lax.ppermute(p1, 'x', ring(X, 3))  4 us
    unnamed x24, local copies, waits for them, and re-layouts  2.92 us
  transfers between devices with their start and end apart: 11, of which 7 were waited for; matrix products, arithmetic and copies ran while one was open for 2% of the time, Pallas kernels for 1%

profile of v1, /device:TPU:8, one launch (start us, length us, event | category | flops | bytes accessed | tf_op | source)
XLA Modules:
  0.0 137.5 jit_solution(4626517258472552210)
XLA Ops:
  0.6 0.0 copy-start
  0.6 0.0 copy-start.1
  0.7 0.0 copy-start.2
  0.7 0.8 copy-done.2
  1.5 0.0 copy-start.4
  1.5 0.7 copy-done.4
  2.2 0.0 copy-start.6
  2.2 0.7 copy-done.6
  2.9 0.0 copy-start.8
  2.9 0.7 copy-done.8
  3.5 0.0 copy-start.10
  3.5 0.0 copy-start.11
  3.5 1.1 shard_map.111
  4.6 21.8 %all-to-all-start = ((bf16[96,16,128]{2,1,0:T(8,128)(2,1)}), bf16[96,16,128]{2,1,0:T(8,128)(2,1)S(1)}, u32[]{:S(2)}, u32[]{:S(2)}) async-start(bf16[96,16,128]{2,1,0:T(8,128)(2,1)} %bitcast.4), calls=%async_computation | async-start | bytes 786432 | tf_op jit(solution)/shard_map/all_to_all | solution.py:188
  26.5 0.0 copy-done
  26.5 1.9 %collective-permute-start.3 = (bf16[192,1536]{1,0:T(8,128)(2,1)S(1)}, bf16[192,1536]{1,0:T(8,128)(2,1)S(1)}, u32[]{:S(2)}, u32[]{:S(2)}) collective-permute-start(bf16[192,1536]{1,0:T(8,128)(2,1)S(1)} %bitcast.22), channel_id=1, source_target_pairs={{0,24},{24,0},{1,25},{25,1},{2,26},{26,2},{3,27},{27,3},{4,28},{28... | collective-permute-start | bytes 1769480 | tf_op jit(solution)/shard_map/ppermute | solution.py:191
  28.4 0.0 copy-done.1
  28.4 2.4 %collective-permute-start.4 = (bf16[192,1536]{1,0:T(8,128)(2,1)S(1)}, bf16[192,1536]{1,0:T(8,128)(2,1)S(1)}, u32[]{:S(2)}, u32[]{:S(2)}) collective-permute-start(bf16[192,1536]{1,0:T(8,128)(2,1)S(1)} %bitcast.24), channel_id=1, source_target_pairs={{0,24},{24,0},{1,25},{25,1},{2,26},{26,2},{3,27},{27,3},{4,28},{28... | collective-permute-start | bytes 1769480 | tf_op jit(solution)/shard_map/ppermute | solution.py:192
  30.8 0.0 copy-done.10
  30.8 0.0 copy-done.11
  30.9 18.3 %all-to-all-done = bf16[96,16,128]{2,1,0:T(8,128)(2,1)S(1)} async-done(((bf16[96,16,128]{2,1,0:T(8,128)(2,1)}), bf16[96,16,128]{2,1,0:T(8,128)(2,1)S(1)}, u32[]{:S(2)}, u32[]{:S(2)}) %all-to-all-start) | async-done | bytes 393248 | tf_op jit(solution)/shard_map/all_to_all | solution.py:188
  49.2 0.4 shard_map.112
  49.6 4.9 %collective-permute-start.2 = (bf16[128,1536]{1,0:T(8,128)(2,1)S(1)}, bf16[128,1536]{1,0:T(8,128)(2,1)S(1)}, u32[]{:S(2)}, u32[]{:S(2)}) collective-permute-start(bf16[128,1536]{1,0:T(8,128)(2,1)S(1)} %get-tuple-element.17.x0), channel_id=1, source_target_pairs={{0,96},{48,144},{96,0},{144,48},{1,97},{49,145},{97,1},{145,49},{2... | collective-permute-start | bytes 1179656 | tf_op jit(solution)/shard_map/ppermute | solution.py:200
  54.5 3.0 %collective-permute-start.1 = (bf16[128,1536]{1,0:T(8,128)(2,1)S(1)}, bf16[128,1536]{1,0:T(8,128)(2,1)S(1)}, u32[]{:S(2)}, u32[]{:S(2)}) collective-permute-start(bf16[128,1536]{1,0:T(8,128)(2,1)S(1)} %get-tuple-element.17.x0), channel_id=1, source_target_pairs={{0,144},{48,0},{96,48},{144,96},{1,145},{49,1},{97,49},{145,97},{2... | collective-permute-start | bytes 1179656 | tf_op jit(solution)/shard_map/ppermute | solution.py:200
  57.6 2.8 %collective-permute-start = (bf16[128,1536]{1,0:T(8,128)(2,1)S(1)}, bf16[128,1536]{1,0:T(8,128)(2,1)S(1)}, u32[]{:S(2)}, u32[]{:S(2)}) collective-permute-start(bf16[128,1536]{1,0:T(8,128)(2,1)S(1)} %get-tuple-element.17.x0), channel_id=1, source_target_pairs={{0,48},{48,96},{96,144},{144,0},{1,49},{49,97},{97,145},{145,1},{2... | collective-permute-start | bytes 1179656 | tf_op jit(solution)/shard_map/ppermute | solution.py:200
  60.4 0.0 collective-permute-done.3.in_sib
  60.4 0.0 collective-permute-done.4.out_sib
  60.4 3.1 %collective-permute-done.2.x3 = bf16[128,1536]{1,0:T(8,128)(2,1)S(1)} collective-permute-done((bf16[128,1536]{1,0:T(8,128)(2,1)S(1)}, bf16[128,1536]{1,0:T(8,128)(2,1)S(1)}, u32[]{:S(2)}, u32[]{:S(2)}) %collective-permute-start.2) | collective-permute-done | bytes 393248 | tf_op jit(solution)/shard_map/ppermute | solution.py:200
  63.5 5.9 %collective-permute-done.1.x2 = bf16[128,1536]{1,0:T(8,128)(2,1)S(1)} collective-permute-done((bf16[128,1536]{1,0:T(8,128)(2,1)S(1)}, bf16[128,1536]{1,0:T(8,128)(2,1)S(1)}, u32[]{:S(2)}, u32[]{:S(2)}) %collective-permute-start.1) | collective-permute-done | bytes 393248 | tf_op jit(solution)/shard_map/ppermute | solution.py:200
  69.4 0.6 collective-permute-done.x1
  70.0 2.6 %shard_map.113 = (f32[64,3072]{1,0:T(8,128)S(1)}, bf16[64,3072]{1,0:T(8,128)(2,1)S(1)}, bf16[64,3072]{1,0:T(8,128)(2,1)S(1)}, bf16[64,3072]{1,0:T(8,128)(2,1)S(1...) custom-call(bf16[128,1536]{1,0:T(8,128)(2,1)S(1)} %get-tuple-element.17.x0, ...), custom_call_target="tpu_custom_call" | custom-call | tf_op jit(solution)/shard_map/pallas_call | solution.py:203
  72.6 1.8 %shard_map.116 = (f32[192,1536]{1,0:T(8,128)S(1)}, f32[192,1536]{1,0:T(8,128)S(1)}, bf16[384,1536]{1,0:T(8,128)(2,1)}) custom-call(bf16[128,1536]{1,0:T(8,128)(2,1)S(1)} %get-tuple-element.17.x0, bf16[128,1536]{1,0:T(8,128)(2,1)S(1)} %collective-permute-done.x1, bf16[128,1536]{1,0:T(8,128)(2,1)S(1)} %collective-permute-done.1.x2, ...), custom_call_target="tpu_custom_call" | custom-call | flops 603979776 | bytes 9437184 | tf_op jit(solution)/shard_map/pallas_call | solution.py:209
  74.4 1.9 %collective-permute-start.8 = (bf16[384,1536]{1,0:T(8,128)(2,1)}, bf16[384,1536]{1,0:T(8,128)(2,1)}, u32[]{:S(2)}, u32[]{:S(2)}) collective-permute-start(bf16[384,1536]{1,0:T(8,128)(2,1)} %get-tuple-element.28), channel_id=1, source_target_pairs={{0,24},{24,0},{1,25},{25,1},{2,26},{26,2},{3,27},{27,3},{4,28},{28... | collective-permute-start | bytes 3538952 | tf_op jit(solution)/shard_map/ppermute | solution.py:219
  76.3 4.0 %collective-permute-start.5 = (bf16[64,3072]{1,0:T(8,128)(2,1)S(1)}, bf16[64,3072]{1,0:T(8,128)(2,1)S(1)}, u32[]{:S(2)}, u32[]{:S(2)}) collective-permute-start(bf16[64,3072]{1,0:T(8,128)(2,1)S(1)} %get-tuple-element.19), channel_id=1, source_target_pairs={{0,144},{48,0},{96,48},{144,96},{1,145},{49,1},{97,49},{145,97},{2... | collective-permute-start | bytes 1179656 | tf_op jit(solution)/shard_map/ppermute | solution.py:206
  80.3 2.7 %collective-permute-start.6 = (bf16[64,3072]{1,0:T(8,128)(2,1)S(1)}, bf16[64,3072]{1,0:T(8,128)(2,1)S(1)}, u32[]{:S(2)}, u32[]{:S(2)}) collective-permute-start(bf16[64,3072]{1,0:T(8,128)(2,1)S(1)} %get-tuple-element.20), channel_id=1, source_target_pairs={{0,96},{48,144},{96,0},{144,48},{1,97},{49,145},{97,1},{145,49},{2... | collective-permute-start | bytes 1179656 | tf_op jit(solution)/shard_map/ppermute | solution.py:208
  83.1 2.8 %collective-permute-start.7 = (bf16[64,3072]{1,0:T(8,128)(2,1)S(1)}, bf16[64,3072]{1,0:T(8,128)(2,1)S(1)}, u32[]{:S(2)}, u32[]{:S(2)}) collective-permute-start(bf16[64,3072]{1,0:T(8,128)(2,1)S(1)} %get-tuple-element.21), channel_id=1, source_target_pairs={{0,48},{48,96},{96,144},{144,0},{1,49},{49,97},{97,145},{145,1},{2... | collective-permute-start | bytes 1179656 | tf_op jit(solution)/shard_map/ppermute | solution.py:207
  85.9 12.0 %collective-permute-done.5.p1 = bf16[64,3072]{1,0:T(8,128)(2,1)S(1)} collective-permute-done((bf16[64,3072]{1,0:T(8,128)(2,1)S(1)}, bf16[64,3072]{1,0:T(8,128)(2,1)S(1)}, u32[]{:S(2)}, u32[]{:S(2)}) %collective-permute-start.5) | collective-permute-done | bytes 393248 | tf_op jit(solution)/shard_map/ppermute | solution.py:206
  97.8 0.0 collective-permute-done.6.p2
  97.8 5.6 %collective-permute-done.7.p3 = bf16[64,3072]{1,0:T(8,128)(2,1)S(1)} collective-permute-done((bf16[64,3072]{1,0:T(8,128)(2,1)S(1)}, bf16[64,3072]{1,0:T(8,128)(2,1)S(1)}, u32[]{:S(2)}, u32[]{:S(2)}) %collective-permute-start.7) | collective-permute-done | bytes 393248 | tf_op jit(solution)/shard_map/ppermute | solution.py:207
  103.4 1.4 shard_map.114
  104.8 8.8 %all-to-all-start.1 = ((bf16[96,16,128]{2,1,0:T(8,128)(2,1)}), bf16[96,16,128]{2,1,0:T(8,128)(2,1)S(1)}, u32[]{:S(2)}, u32[]{:S(2)}) async-start(bf16[96,16,128]{2,1,0:T(8,128)(2,1)} %bitcast.10), calls=%async_computation.1 | async-start | bytes 786432 | tf_op jit(solution)/shard_map/all_to_all | solution.py:188
  113.6 0.0 collective-permute-done.8
  113.6 1.5 %convert_element_type.3 = f32[384,1536]{1,0:T(8,128)S(1)} convert(bf16[384,1536]{1,0:T(8,128)(2,1)} %collective-permute-done.8) | non-fusion elementwise | flops 589824 | bytes 3538944 | tf_op jit(solution)/shard_map/convert_element_type | solution.py:219
  115.1 0.0 copy-start.3
  115.1 0.0 copy-start.5
  115.1 0.0 copy-start.7
  115.2 0.0 copy-start.9
  115.2 1.8 %fusion = (f32[1,192,1536]{2,1,0:T(8,128)}, f32[1,1536,192]{1,2,0:T(8,128)}) fusion(f32[192,1536]{1,0:T(8,128)S(1)} %get-tuple-element.29, f32[384,1536]{1,0:T(8,128)S(1)} %convert_element_type.3, f32[192,1536]{1,0:T(8,128)S(1)} %get-tuple-element.27), kind=kLoop, calls=%fused_computation.1 | loop fusion | flops 589824 | bytes 7077888 | tf_op jit(solution)/shard_map/broadcast_in_dim | solution.py:227
  117.0 19.5 %all-to-all-done.1 = bf16[96,16,128]{2,1,0:T(8,128)(2,1)S(1)} async-done(((bf16[96,16,128]{2,1,0:T(8,128)(2,1)}), bf16[96,16,128]{2,1,0:T(8,128)(2,1)S(1)}, u32[]{:S(2)}, u32[]{:S(2)}) %all-to-all-start.1) | async-done | bytes 393248 | tf_op jit(solution)/shard_map/all_to_all | solution.py:188
  136.5 0.0 copy-done.3
  136.5 0.0 copy-done.5
  136.5 0.0 copy-done.7
  136.5 0.0 copy-done.9
  136.5 1.0 shard_map.115
  (2 shorter events, 0.0 us)
Async XLA Ops:
  0.6 25.8 %copy-start = (bf16[1,1536,192]{1,2,0:T(8,128)(2,1)S(1)}, bf16[1,1536,192]{1,2,0:T(8,128)(2,1)}, u32[]{:S(2)}) copy-start(bf16[1,1536,192]{1,2,0:T(8,128)(2,1)} %param.14) | copy-start | bytes 1769476
  0.6 27.8 %copy-start.1 = (bf16[1,192,1536]{2,1,0:T(8,128)(2,1)S(1)}, bf16[1,192,1536]{2,1,0:T(8,128)(2,1)}, u32[]{:S(2)}) copy-start(bf16[1,192,1536]{2,1,0:T(8,128)(2,1)} %param.15) | copy-start | bytes 1769476
  0.7 0.8 copy-start.2
  1.5 0.7 copy-start.4
  2.2 0.7 copy-start.6
  2.9 0.7 copy-start.8
  3.5 27.3 %copy-start.10 = (f32[1536]{0:T(1024)S(1)}, f32[1536]{0:T(1024)}, u32[]{:S(2)}) copy-start(f32[1536]{0:T(1024)} %param.12) | copy-start | bytes 18436
  3.5 27.3 %copy-start.11 = (f32[1536]{0:T(1024)S(1)}, f32[1536]{0:T(1024)}, u32[]{:S(2)}) copy-start(f32[1536]{0:T(1024)} %param.13) | copy-start | bytes 18436
  4.6 44.6 %all-to-all-start = ((bf16[96,16,128]{2,1,0:T(8,128)(2,1)}), bf16[96,16,128]{2,1,0:T(8,128)(2,1)S(1)}, u32[]{:S(2)}, u32[]{:S(2)}) async-start(bf16[96,16,128]{2,1,0:T(8,128)(2,1)} %bitcast.4), calls=%async_computation | async-start | bytes 786432 | tf_op jit(solution)/shard_map/all_to_all | solution.py:188
  26.5 33.9 %collective-permute-start.3 = (bf16[192,1536]{1,0:T(8,128)(2,1)S(1)}, bf16[192,1536]{1,0:T(8,128)(2,1)S(1)}, u32[]{:S(2)}, u32[]{:S(2)}) collective-permute-start(bf16[192,1536]{1,0:T(8,128)(2,1)S(1)} %bitcast.22), channel_id=1, source_target_pairs={{0,24},{24,0},{1,25},{25,1},{2,26},{26,2},{3,27},{27,3},{4,28},{28... | collective-permute-start | bytes 1769480 | tf_op jit(solution)/shard_map/ppermute | solution.py:191
  28.4 32.0 %collective-permute-start.4 = (bf16[192,1536]{1,0:T(8,128)(2,1)S(1)}, bf16[192,1536]{1,0:T(8,128)(2,1)S(1)}, u32[]{:S(2)}, u32[]{:S(2)}) collective-permute-start(bf16[192,1536]{1,0:T(8,128)(2,1)S(1)} %bitcast.24), channel_id=1, source_target_pairs={{0,24},{24,0},{1,25},{25,1},{2,26},{26,2},{3,27},{27,3},{4,28},{28... | collective-permute-start | bytes 1769480 | tf_op jit(solution)/shard_map/ppermute | solution.py:192
  49.6 13.9 %collective-permute-start.2 = (bf16[128,1536]{1,0:T(8,128)(2,1)S(1)}, bf16[128,1536]{1,0:T(8,128)(2,1)S(1)}, u32[]{:S(2)}, u32[]{:S(2)}) collective-permute-start(bf16[128,1536]{1,0:T(8,128)(2,1)S(1)} %get-tuple-element.17.x0), channel_id=1, source_target_pairs={{0,96},{48,144},{96,0},{144,48},{1,97},{49,145},{97,1},{145,49},{2... | collective-permute-start | bytes 1179656 | tf_op jit(solution)/shard_map/ppermute | solution.py:200
  54.5 14.8 %collective-permute-start.1 = (bf16[128,1536]{1,0:T(8,128)(2,1)S(1)}, bf16[128,1536]{1,0:T(8,128)(2,1)S(1)}, u32[]{:S(2)}, u32[]{:S(2)}) collective-permute-start(bf16[128,1536]{1,0:T(8,128)(2,1)S(1)} %get-tuple-element.17.x0), channel_id=1, source_target_pairs={{0,144},{48,0},{96,48},{144,96},{1,145},{49,1},{97,49},{145,97},{2... | collective-permute-start | bytes 1179656 | tf_op jit(solution)/shard_map/ppermute | solution.py:200
  57.6 12.4 %collective-permute-start = (bf16[128,1536]{1,0:T(8,128)(2,1)S(1)}, bf16[128,1536]{1,0:T(8,128)(2,1)S(1)}, u32[]{:S(2)}, u32[]{:S(2)}) collective-permute-start(bf16[128,1536]{1,0:T(8,128)(2,1)S(1)} %get-tuple-element.17.x0), channel_id=1, source_target_pairs={{0,48},{48,96},{96,144},{144,0},{1,49},{49,97},{97,145},{145,1},{2... | collective-permute-start | bytes 1179656 | tf_op jit(solution)/shard_map/ppermute | solution.py:200
  74.4 39.1 %collective-permute-start.8 = (bf16[384,1536]{1,0:T(8,128)(2,1)}, bf16[384,1536]{1,0:T(8,128)(2,1)}, u32[]{:S(2)}, u32[]{:S(2)}) collective-permute-start(bf16[384,1536]{1,0:T(8,128)(2,1)} %get-tuple-element.28), channel_id=1, source_target_pairs={{0,24},{24,0},{1,25},{25,1},{2,26},{26,2},{3,27},{27,3},{4,28},{28... | collective-permute-start | bytes 3538952 | tf_op jit(solution)/shard_map/ppermute | solution.py:219
  76.3 21.5 %collective-permute-start.5 = (bf16[64,3072]{1,0:T(8,128)(2,1)S(1)}, bf16[64,3072]{1,0:T(8,128)(2,1)S(1)}, u32[]{:S(2)}, u32[]{:S(2)}) collective-permute-start(bf16[64,3072]{1,0:T(8,128)(2,1)S(1)} %get-tuple-element.19), channel_id=1, source_target_pairs={{0,144},{48,0},{96,48},{144,96},{1,145},{49,1},{97,49},{145,97},{2... | collective-permute-start | bytes 1179656 | tf_op jit(solution)/shard_map/ppermute | solution.py:206
  80.3 17.5 %collective-permute-start.6 = (bf16[64,3072]{1,0:T(8,128)(2,1)S(1)}, bf16[64,3072]{1,0:T(8,128)(2,1)S(1)}, u32[]{:S(2)}, u32[]{:S(2)}) collective-permute-start(bf16[64,3072]{1,0:T(8,128)(2,1)S(1)} %get-tuple-element.20), channel_id=1, source_target_pairs={{0,96},{48,144},{96,0},{144,48},{1,97},{49,145},{97,1},{145,49},{2... | collective-permute-start | bytes 1179656 | tf_op jit(solution)/shard_map/ppermute | solution.py:208
  83.1 20.3 %collective-permute-start.7 = (bf16[64,3072]{1,0:T(8,128)(2,1)S(1)}, bf16[64,3072]{1,0:T(8,128)(2,1)S(1)}, u32[]{:S(2)}, u32[]{:S(2)}) collective-permute-start(bf16[64,3072]{1,0:T(8,128)(2,1)S(1)} %get-tuple-element.21), channel_id=1, source_target_pairs={{0,48},{48,96},{96,144},{144,0},{1,49},{49,97},{97,145},{145,1},{2... | collective-permute-start | bytes 1179656 | tf_op jit(solution)/shard_map/ppermute | solution.py:207
  104.8 31.7 %all-to-all-start.1 = ((bf16[96,16,128]{2,1,0:T(8,128)(2,1)}), bf16[96,16,128]{2,1,0:T(8,128)(2,1)S(1)}, u32[]{:S(2)}, u32[]{:S(2)}) async-start(bf16[96,16,128]{2,1,0:T(8,128)(2,1)} %bitcast.10), calls=%async_computation.1 | async-start | bytes 786432 | tf_op jit(solution)/shard_map/all_to_all | solution.py:188
  115.1 21.4 %copy-start.3 = (bf16[128,64]{0,1:T(8,128)(2,1)S(1)}, bf16[128,64]{0,1:T(8,128)(2,1)}, u32[]{:S(2)}) copy-start(bf16[128,64]{0,1:T(8,128)(2,1)} %param.8) | copy-start | bytes 49156
  115.1 21.3 %copy-start.5 = (bf16[128,64]{0,1:T(8,128)(2,1)S(1)}, bf16[128,64]{0,1:T(8,128)(2,1)}, u32[]{:S(2)}) copy-start(bf16[128,64]{0,1:T(8,128)(2,1)} %param.9) | copy-start | bytes 49156
  115.1 21.3 %copy-start.7 = (s32[128,2]{0,1:T(2,128)S(1)}, s32[128,2]{0,1:T(2,128)}, u32[]{:S(2)}) copy-start(s32[128,2]{0,1:T(2,128)} %param.10) | copy-start | bytes 3076
  115.2 21.3 %copy-start.9 = (f32[128,2]{0,1:T(2,128)S(1)}, f32[128,2]{0,1:T(2,128)}, u32[]{:S(2)}) copy-start(f32[128,2]{0,1:T(2,128)} %param.11) | copy-start | bytes 3076

commit v2 on v1

v2 whole, which is shorter than its diff:
```python
import jax
import jax.numpy as jnp
from jax import lax
from jax.experimental import pallas as pl
from jax.experimental.pallas import tpu as pltpu
from jax.sharding import Mesh
from jax.sharding import PartitionSpec as P

epsilon = 1e-05
LANES = 128
HALF = 64
Y_FAR, Y_NEAR, X_HI, X_LO, CORE, Y_HI, Z = 2, 2, 2, 2, 2, 2, 12
EXPERTS = Y_HI * Z
CAP = 16
SLOTS = EXPERTS * CAP
ROWS = Y_FAR * CAP
GROUP = Y_NEAR * X_HI
DP_AXES = ("yfar", "ynear", "xhi", "xlo", "core")
EXPERT_AXES = ("yh", "z")
SWAP = [(0, 1), (1, 0)]
MIB = 1024 * 1024
F32 = jnp.float32
VMEM, ANY = pltpu.VMEM, pl.ANY
DMA = pltpu.SemaphoreType.DMA
BF16 = jnp.bfloat16


def call(kernel, out_shapes, flops=0, bytes_accessed=0, vmem=6, **more):
    return pl.pallas_call(
        kernel,
        out_shape=out_shapes,
        compiler_params=pltpu.CompilerParams(vmem_limit_bytes=vmem * MIB),
        cost_estimate=pl.CostEstimate(
            flops=flops, bytes_accessed=bytes_accessed, transcendentals=0
        ),
        **more,
    )


def spaces(*names):
    return [pl.BlockSpec(memory_space=name) for name in names]


def dot(a, b, ca, cb):
    return lax.dot_general(a, b, (((ca,), (cb,)), ((), ())), preferred_element_type=F32)


def places(routes):
    tokens = routes.shape[1]
    first, second = routes[0:1], routes[1:2]
    experts = lax.broadcasted_iota(jnp.int32, (EXPERTS, tokens), 0)
    names = (experts == first, experts == second)
    either = (names[0] | names[1]).astype(F32)
    before = lax.broadcasted_iota(jnp.int32, (tokens, tokens), 0) < lax.broadcasted_iota(
        jnp.int32, (tokens, tokens), 1
    )
    earlier = dot(either.astype(BF16), before.astype(F32).astype(BF16), 1, 0)
    rows = lax.broadcasted_iota(jnp.int32, (SLOTS, tokens), 0)
    masks = []
    for name, expert in zip(names, (first, second)):
        slot = jnp.sum(jnp.where(name, earlier, 0.0), axis=0, keepdims=True)
        masks.append(rows == expert * CAP + slot.astype(jnp.int32))
    return masks


def route_kernel(routes_ref, gates_ref, frames_ref, cotangent_ref, out_ref):
    mask0, mask1 = places(routes_ref[...])
    gates = 0.5 * gates_ref[...]
    scale = jnp.sum(
        jnp.where(mask0, gates[0:1], 0.0) + jnp.where(mask1, gates[1:2], 0.0),
        axis=1,
        keepdims=True,
    )
    chosen = (mask0 | mask1).astype(F32).astype(BF16)
    both = jnp.concatenate([frames_ref[...], cotangent_ref[...]], axis=0)
    picked = dot(chosen, both, 1, 1)
    lane = lax.broadcasted_iota(jnp.int32, picked.shape, 1)
    sent = jnp.where(lane < HALF, picked, picked * scale).astype(BF16)
    sent = sent.reshape(EXPERTS, CAP, LANES)
    for y in range(Y_FAR):
        out_ref[y] = sent


def swap_halves(a):
    return pltpu.roll(a, HALF, 1)


def normal(rows):
    mean = jnp.mean(rows, axis=-1, keepdims=True)
    centered = rows - mean
    var = jnp.mean(centered * centered, axis=-1, keepdims=True)
    scaled = lax.rsqrt(var + epsilon)
    return centered * scaled, scaled


def normalize_kernel(came_ref, gain_ref, bias_ref, sent_ref, rows_ref, values_ref):
    lane = lax.broadcasted_iota(jnp.int32, (ROWS, LANES), 1)
    for p in range(EXPERTS // 2):
        a = came_ref[:, 2 * p].astype(F32).reshape(ROWS, LANES)
        b = came_ref[:, 2 * p + 1].astype(F32).reshape(ROWS, LANES)
        cols = slice(p * LANES, (p + 1) * LANES)
        values_ref[:, cols] = jnp.where(lane < HALF, a, swap_halves(b))
        grads = jnp.where(lane < HALF, swap_halves(a), b).astype(BF16)
        for g in range(GROUP):
            sent_ref[g, ROWS:, cols] = grads
    values = values_ref[...]
    rows_ref[...] = values.astype(BF16)
    unit, _ = normal(values)
    normed = (unit * gain_ref[...] + bias_ref[...]).astype(BF16)
    for g in range(GROUP):
        sent_ref[g, :ROWS] = normed


def gathered(x, first):
    return jnp.concatenate([x[g, first : first + ROWS] for g in range(GROUP)], axis=0)


def expert_kernel(x, w0, w1, w2, w3, part_ref, hid_ref, back_ref, v2, v3, sems):
    width = x.shape[2]
    units = w0.shape[0] // 2
    loads = [
        pltpu.make_async_copy(w, v, sems.at[i]) for i, (w, v) in enumerate(((w2, v2), (w3, v3)))
    ]
    for load in loads:
        load.start()
    normed = gathered(x, 0)
    grads = gathered(x, ROWS)
    forward, backward = 0.0, 0.0
    for i, w in enumerate((w0, w1, v2, v3)):
        if i >= 2:
            loads[i - 2].wait()
        weight_in, weight_out = w[:units], w[units:]
        inner = dot(normed, weight_in, 1, 1)
        back_hidden = dot(grads, weight_out, 1, 1)
        sigm = jax.nn.sigmoid(inner)
        hidden = (inner * sigm).astype(BF16)
        back_inner = (back_hidden * sigm * (1.0 + inner * (1.0 - sigm))).astype(BF16)
        hid_ref[i] = hidden
        back_ref[i] = back_inner
        forward += dot(hidden, weight_out, 1, 0)
        backward += dot(back_inner, weight_in, 1, 0)
    for g in range(GROUP):
        rows = slice(g * ROWS, (g + 1) * ROWS)
        part_ref[g, :, :width] = forward[rows].astype(BF16)
        part_ref[g, :, width:] = backward[rows].astype(BF16)


def grad_pair(x, hid_ref, back_ref, i):
    return (
        dot(back_ref[i], gathered(x, 0), 0, 0),
        dot(hid_ref[i], gathered(x, ROWS), 0, 0),
    )


def grads_kernel(x, hid_ref, back_ref, sib_ref):
    units = hid_ref.shape[2]
    for i in (2, 3):
        base = (i - 2) * 2 * units
        grad_in, grad_out = grad_pair(x, hid_ref, back_ref, i)
        sib_ref[base : base + units] = grad_in.astype(BF16)
        sib_ref[base + units : base + 2 * units] = grad_out.astype(BF16)


def fold_kernel(x, hid_ref, back_ref, came_ref, send_ref):
    units = hid_ref.shape[2]
    grad_in, grad_out = grad_pair(x, hid_ref, back_ref, 1)
    base = 2 * units
    send_ref[:units] = (grad_in + came_ref[base : base + units].astype(F32)).astype(BF16)
    send_ref[units:] = (grad_out + came_ref[base + units :].astype(F32)).astype(BF16)


def finish_kernel(x, hid_ref, back_ref, came_ref, far_ref, in_any, out_any, in_ref, out_ref, sems):
    units = hid_ref.shape[2]
    copies = []
    sources = ((back_ref, 0, in_ref, in_any), (hid_ref, ROWS, out_ref, out_any))
    for i, (left, first, ref, whole) in enumerate(sources):
        rows = slice(i * units, (i + 1) * units)
        own = dot(left[0], gathered(x, first), 0, 0)
        ref[...] = own + came_ref[rows].astype(F32) + far_ref[rows].astype(F32)
        copies.append(pltpu.make_async_copy(ref, whole, sems.at[i]))
        copies[i].start()
    for copy in copies:
        copy.wait()


def back_kernel(part_ref, rows_ref, gain_ref, out_ref):
    width = rows_ref.shape[1]

    def total(cols):
        parts = [part_ref[g, :, cols].astype(F32) for g in range(GROUP)]
        return (parts[0] + parts[1]) + (parts[2] + parts[3])

    unit, scaled = normal(rows_ref[...].astype(F32))
    back_unit = total(slice(width, 2 * width)) * gain_ref[...]
    first = jnp.mean(back_unit, axis=-1, keepdims=True)
    second = jnp.mean(back_unit * unit, axis=-1, keepdims=True)
    back = (back_unit - first - unit * second) * scaled
    lane = lax.broadcasted_iota(jnp.int32, (ROWS, LANES), 1)
    for p in range(EXPERTS // 2):
        cols = slice(p * LANES, (p + 1) * LANES)
        a, b = total(cols), back[:, cols]
        low = jnp.where(lane < HALF, a, swap_halves(b))
        high = jnp.where(lane < HALF, swap_halves(a), b)
        out_ref[:, 2 * p] = low.astype(BF16).reshape(Y_FAR, CAP, LANES)
        out_ref[:, 2 * p + 1] = high.astype(BF16).reshape(Y_FAR, CAP, LANES)


def combine_kernel(came_ref, routes_ref, gates_ref, frames_ref, cotangent_ref, out_ref, fg_ref):
    total = came_ref[0].astype(F32)
    for y in range(1, Y_FAR):
        total = total + came_ref[y].astype(F32)
    came = total.astype(BF16).reshape(SLOTS, LANES)
    gates = 0.5 * gates_ref[...]
    taken = [dot(came, mask.astype(F32).astype(BF16), 0, 0) for mask in places(routes_ref[...])]
    results = taken[0][:HALF] * gates[0:1] + taken[1][:HALF] * gates[1:2]
    backs = taken[0][HALF:] + taken[1][HALF:]
    out_ref[...] = (frames_ref[...].astype(F32) + results).astype(BF16)
    fg_ref[...] = (cotangent_ref[...].astype(F32) + backs).astype(BF16)


def body(frames, cotangent, routes, route_gates, norm_gain, norm_bias, expert_in, expert_out):
    width = norm_gain.shape[0]
    units = expert_out.shape[1]
    frames_t, cotangent_t = frames.T, cotangent.T
    routes_t, gates_t = routes.T, route_gates.T
    gain, bias = norm_gain[None], norm_bias[None]
    in_own, out_own = expert_in[0].T, expert_out[0]
    shape = jax.ShapeDtypeStruct
    blocks = shape((Y_FAR, EXPERTS, CAP, LANES), BF16)

    def exchange(a):
        a = a.reshape(Y_FAR * EXPERTS, CAP, LANES)
        a = lax.all_to_all(a, ("yfar",) + EXPERT_AXES, split_axis=0, concat_axis=0, tiled=True)
        return a.reshape(Y_FAR, EXPERTS, CAP, LANES)

    w0 = jnp.concatenate([in_own, out_own], axis=0)
    w1 = lax.ppermute(w0, "xlo", SWAP)
    w2 = lax.ppermute(w0, "core", SWAP)
    came = exchange(call(route_kernel, blocks)(routes_t, gates_t, frames_t, cotangent_t))
    came, w1 = lax.optimization_barrier((came, w1))
    w3 = lax.ppermute(w1, "core", SWAP)
    spread, rows = call(
        normalize_kernel,
        (shape((GROUP, 2 * ROWS, width), BF16), shape((ROWS, width), BF16)),
        scratch_shapes=[VMEM((ROWS, width), F32)],
    )(came, gain, bias)

    def group(a):
        return lax.all_to_all(a, ("ynear", "xhi"), split_axis=0, concat_axis=0, tiled=True)

    x = group(spread)
    kept = shape((4, GROUP * ROWS, units), BF16)
    stack = (2 * units, width)
    work = 4 * GROUP * ROWS * units * width
    parts, hidden, back_inner = call(
        expert_kernel,
        (shape((GROUP, ROWS, 2 * width), BF16), kept, kept),
        flops=8 * work,
        bytes_accessed=16 * units * width,
        vmem=16,
        in_specs=spaces(VMEM, VMEM, VMEM, ANY, ANY),
        scratch_shapes=[VMEM(stack, BF16), VMEM(stack, BF16), DMA((2,))],
    )(x, w0, w1, w2, w3)
    came_parts = group(parts)
    for_sib = call(
        grads_kernel,
        shape((4 * units, width), BF16),
        flops=2 * work,
        bytes_accessed=8 * units * width,
        vmem=12,
    )(x, hidden, back_inner)
    from_sib = lax.ppermute(for_sib, "core", SWAP)
    came_parts, from_sib = lax.optimization_barrier((came_parts, from_sib))
    for_far = call(
        fold_kernel,
        shape(stack, BF16),
        flops=work,
        bytes_accessed=8 * units * width,
        vmem=12,
    )(x, hidden, back_inner, from_sib)
    from_far = lax.ppermute(for_far, "xlo", SWAP)
    grad = shape((units, width), F32)
    grad_in, grad_out = call(
        finish_kernel,
        (grad, grad),
        flops=work,
        bytes_accessed=16 * units * width,
        vmem=12,
        out_specs=spaces(ANY, ANY),
        scratch_shapes=[VMEM((units, width), F32), VMEM((units, width), F32), DMA((2,))],
    )(x, hidden, back_inner, from_sib, from_far)
    backs = exchange(call(back_kernel, blocks)(came_parts, rows, gain))
    token = shape(frames_t.shape, BF16)
    output, frame_grads = call(combine_kernel, (token, token))(
        backs, routes_t, gates_t, frames_t, cotangent_t
    )
    return (output.T, frame_grads.T, grad_in.T[None], grad_out[None])


def solution(mesh):
    fine = Mesh(mesh.devices.reshape(Y_FAR, Y_NEAR, X_HI, X_LO, CORE, Y_HI, Z), DP_AXES + EXPERT_AXES)
    tokens = P(DP_AXES, EXPERT_AXES)
    weights_in = P(EXPERT_AXES, None, DP_AXES)
    weights_out = P(EXPERT_AXES, DP_AXES, None)
    return jax.shard_map(
        body,
        mesh=fine,
        in_specs=(
            tokens,
            tokens,
            P(DP_AXES, None),
            P(DP_AXES, None),
            P(),
            P(),
            weights_in,
            weights_out,
        ),
        out_specs=(tokens, tokens, weights_in, weights_out),
        check_vma=False,
    )
```

time: 138 us -> 115 us (0.83)
  the two profiles are of different devices: /device:TPU:8 before, /device:TPU:2 now
where the time goes in v2:
time: 115 us
  blocking collectives  42.6 us (37%)
  starting transfers between devices  36.8 us (32%)
  waiting for transfers between devices  23.7 us (21%)
  Pallas kernels  8.72 us (8%)
  other arithmetic  1.35 us (1%)
    all_to_all x1, blocking collectives, exchange(): lax.all_to_all(a, ('yfar',) + EXPERT_AXES, split_axis=0, concat_axis=0, t...  26.4 us
    all_to_all x1, blocking collectives, group(): lax.all_to_all(a, ('ynear', 'xhi'), split_axis=0, concat_axis=0, tiled=True)  16.2 us
    all_to_all x1, waiting for transfers between devices, exchange(): lax.all_to_all(a, ('yfar',) + EXPERT_AXES, split_axis=0, concat_axis=0, t...  15.9 us
    all_to_all x1, starting transfers between devices, exchange(): lax.all_to_all(a, ('yfar',) + EXPERT_AXES, split_axis=0, concat_axis=0, t...  12.1 us
    ppermute x1, starting transfers between devices, body(): w1 = lax.ppermute(w0, 'xlo', SWAP)  11.5 us
    all_to_all x1, waiting for transfers between devices, group(): lax.all_to_all(a, ('ynear', 'xhi'), split_axis=0, concat_axis=0, tiled=True)  7.74 us
    all_to_all x1, starting transfers between devices, group(): lax.all_to_all(a, ('ynear', 'xhi'), split_axis=0, concat_axis=0, tiled=True)  3.81 us
    ppermute x1, starting transfers between devices, body(): from_far = lax.ppermute(for_far, 'xlo', SWAP)  3.72 us
  transfers between devices with their start and end apart: 7, of which 2 were waited for; matrix products, arithmetic and copies ran while one was open for 0% of the time, Pallas kernels for 2%

profile of v2, /device:TPU:2, one launch (start us, length us, event | category | flops | bytes accessed | tf_op | source)
XLA Modules:
  0.0 115.0 jit_solution(586261739295633376)
XLA Ops:
  0.6 0.0 copy-start.1
  0.6 0.0 copy-start.2
  0.7 0.0 copy-start.3
  0.7 0.0 copy-start.4
  0.7 0.0 copy-start.5
  0.7 0.0 copy-start.6
  0.7 1.4 %pad_maximum_fusion.w0 = bf16[384,1536]{1,0:T(8,128)(2,1)S(1)} fusion(bf16[192,1536]{1,0:T(8,128)(2,1)} %bitcast.29, bf16[192,1536]{1,0:T(8,128)(2,1)} %bitcast.30), kind=kLoop, calls=%fused_computation | loop fusion | flops 2359296 | bytes 2359296 | tf_op jit(solution)/shard_map/concatenate | solution.py:236
  2.0 11.5 %collective-permute-start = (bf16[384,1536]{1,0:T(8,128)(2,1)S(1)}, bf16[384,1536]{1,0:T(8,128)(2,1)S(1)}, u32[]{:S(2)}, u32[]{:S(2)}) collective-permute-start(bf16[384,1536]{1,0:T(8,128)(2,1)S(1)} %pad_maximum_fusion.w0), channel_id=1, source_target_pairs={{0,48},{48,0},{1,49},{49,1},{2,50},{50,2},{3,51},{51,3},{4,52},{52... | collective-permute-start | bytes 3538952 | tf_op jit(solution)/shard_map/ppermute | solution.py:237
  13.5 0.0 copy-done.1
  13.5 0.0 copy-done.2
  13.5 0.0 copy-done.3
  13.5 0.0 copy-done.4
  13.6 1.0 shard_map.111
  14.6 12.1 %all-to-all-start = ((bf16[48,16,128]{2,1,0:T(8,128)(2,1)}), bf16[48,16,128]{2,1,0:T(8,128)(2,1)S(1)}, u32[]{:S(2)}, u32[]{:S(2)}) async-start(bf16[48,16,128]{2,1,0:T(8,128)(2,1)} %bitcast.4), calls=%async_computation | async-start | bytes 393216 | tf_op jit(solution)/shard_map/all_to_all | solution.py:233
  26.7 1.9 %collective-permute-start.1 = (bf16[384,1536]{1,0:T(8,128)(2,1)S(1)}, bf16[384,1536]{1,0:T(8,128)(2,1)}, u32[]{:S(2)}, u32[]{:S(2)}) collective-permute-start(bf16[384,1536]{1,0:T(8,128)(2,1)S(1)} %pad_maximum_fusion.w0), channel_id=1, source_target_pairs={{0,24},{24,0},{1,25},{25,1},{2,26},{26,2},{3,27},{27,3},{4,28},{28... | collective-permute-start | bytes 3538952 | tf_op jit(solution)/shard_map/ppermute | solution.py:238
  28.6 0.0 copy-done.5
  28.6 0.0 copy-done.6
  28.6 15.9 %all-to-all-done = bf16[48,16,128]{2,1,0:T(8,128)(2,1)S(1)} async-done(((bf16[48,16,128]{2,1,0:T(8,128)(2,1)}), bf16[48,16,128]{2,1,0:T(8,128)(2,1)S(1)}, u32[]{:S(2)}, u32[]{:S(2)}) %all-to-all-start) | async-done | bytes 196640 | tf_op jit(solution)/shard_map/all_to_all | solution.py:233
  44.6 0.0 collective-permute-done.w1
  44.6 0.3 shard_map.112
  44.9 0.0 copy-start
  44.9 0.9 copy-done
  45.8 3.8 %all-to-all-start.1 = ((bf16[4,64,1536]{2,1,0:T(8,128)(2,1)}), bf16[4,64,1536]{2,1,0:T(8,128)(2,1)S(1)}, u32[]{:S(2)}, u32[]{:S(2)}) async-start(bf16[4,64,1536]{2,1,0:T(8,128)(2,1)} %copy-done), calls=%async_computation.1 | async-start | bytes 1572864 | tf_op jit(solution)/shard_map/all_to_all | solution.py:249
  49.6 1.9 %collective-permute-start.2 = (bf16[384,1536]{1,0:T(8,128)(2,1)S(1)}, bf16[384,1536]{1,0:T(8,128)(2,1)}, u32[]{:S(2)}, u32[]{:S(2)}) collective-permute-start(bf16[384,1536]{1,0:T(8,128)(2,1)S(1)} %collective-permute-done.w1), channel_id=1, source_target_pairs={{0,24},{24,0},{1,25},{25,1},{2,26},{26,2},{3,27},{27,3},{4,28},{28... | collective-permute-start | bytes 3538952 | tf_op jit(solution)/shard_map/ppermute | solution.py:241
  51.5 0.0 collective-permute-done.1.w2
  51.5 7.7 %all-to-all-done.1.x = bf16[4,64,1536]{2,1,0:T(8,128)(2,1)S(1)} async-done(((bf16[4,64,1536]{2,1,0:T(8,128)(2,1)}), bf16[4,64,1536]{2,1,0:T(8,128)(2,1)S(1)}, u32[]{:S(2)}, u32[]{:S(2)}) %all-to-all-start.1) | async-done | bytes 786464 | tf_op jit(solution)/shard_map/all_to_all | solution.py:249
  59.3 0.0 collective-permute-done.2.w3
  59.3 2.9 %shard_map.113 = (bf16[4,32,3072]{2,1,0:T(8,128)(2,1)S(1)}, bf16[4,128,192]{2,1,0:T(8,128)(2,1)S(1)}, bf16[4,128,192]{2,1,0:T(8,128)(2,1)S(1)}) custom-call(bf16[4,64,1536]{2,1,0:T(8,128)(2,1)S(1)} %all-to-all-done.1.x, bf16[384,1536]{1,0:T(8,128)(2,1)S(1)} %pad_maximum_fusion.w0, bf16[384,1536]{1,0:T(8,128)(2,1)S(1)} %collective-permute-done.w1, ...), custom_call_target="tpu_custom_call" | custom-call | flops 1207959552 | bytes 4718592 | tf_op jit(solution)/shard_map/pallas_call | solution.py:255
  62.2 0.8 shard_map.114
  63.0 1.9 %collective-permute-start.3 = (bf16[768,1536]{1,0:T(8,128)(2,1)S(1)}, bf16[768,1536]{1,0:T(8,128)(2,1)S(1)}, u32[]{:S(2)}, u32[]{:S(2)}) collective-permute-start(bf16[768,1536]{1,0:T(8,128)(2,1)S(1)} %shard_map.114), channel_id=1, source_target_pairs={{0,24},{24,0},{1,25},{25,1},{2,26},{26,2},{3,27},{27,3},{4,28},{28... | collective-permute-start | bytes 7077896 | tf_op jit(solution)/shard_map/ppermute | solution.py:272
  65.0 16.2 %all_to_all.20.part_ref = bf16[4,32,3072]{2,1,0:T(8,128)(2,1)S(1)} all-to-all(bf16[4,32,3072]{2,1,0:T(8,128)(2,1)S(1)} %get-tuple-element.20), channel_id=1, replica_groups=mesh['yfar'=2,'ynear'=2,'xhi'=2,'xlo'=2,'core'=2,'yh'=2,'z'=12] {'ynear'..., dimensions={0} | all-to-all | bytes 1572864 | tf_op jit(solution)/shard_map/all_to_all | solution.py:249
  81.1 0.0 collective-permute-done.3.came_ref
  81.1 0.5 shard_map.117
  81.6 3.7 %collective-permute-start.4 = (bf16[384,1536]{1,0:T(8,128)(2,1)S(1)}, bf16[384,1536]{1,0:T(8,128)(2,1)S(1)}, u32[]{:S(2)}, u32[]{:S(2)}) collective-permute-start(bf16[384,1536]{1,0:T(8,128)(2,1)S(1)} %shard_map.117), channel_id=1, source_target_pairs={{0,48},{48,0},{1,49},{49,1},{2,50},{50,2},{3,51},{51,3},{4,52},{52... | collective-permute-start | bytes 3538952 | tf_op jit(solution)/shard_map/ppermute | solution.py:281
  85.4 0.4 shard_map.115
  85.8 26.4 %all_to_all.21 = bf16[48,16,128]{2,1,0:T(8,128)(2,1)S(1)} all-to-all(bf16[48,16,128]{2,1,0:T(8,128)(2,1)S(1)} %bitcast.20), channel_id=1, replica_groups=mesh['yfar'=2,'ynear'=2,'xhi'=2,'xlo'=2,'core'=2,'yh'=2,'z'=12] {'yfar',..., dimensions={0} | all-to-all | bytes 393216 | tf_op jit(solution)/shard_map/all_to_all | solution.py:233
  112.3 1.0 shard_map.116
  113.2 0.0 collective-permute-done.4.far_ref
  113.2 1.8 %shard_map.118 = (f32[192,1536]{1,0:T(8,128)}, f32[192,1536]{1,0:T(8,128)}) custom-call(bf16[4,64,1536]{2,1,0:T(8,128)(2,1)S(1)} %all-to-all-done.1.x, bf16[4,128,192]{2,1,0:T(8,128)(2,1)S(1)} %get-tuple-element.21.hid_ref, bf16[4,128,192]{2,1,0:T(8,128)(2,1)S(1)} %get-tuple-element.22.back_ref, bf16[768,1536]{1,0:T(8,128)(2,1)S(1)} %collective-permute-done.3.came_ref, ...), custom_call_target="tpu_custom_call" | custom-call | flops 150994944 | bytes 4718592 | tf_op jit(solution)/shard_map/pallas_call | solution.py:283
  (2 shorter events, 0.0 us)
Async XLA Ops:
  0.6 12.9 %copy-start.1 = (bf16[128,64]{0,1:T(8,128)(2,1)S(1)}, bf16[128,64]{0,1:T(8,128)(2,1)}, u32[]{:S(2)}) copy-start(bf16[128,64]{0,1:T(8,128)(2,1)} %param.8) | copy-start | bytes 49156
  0.6 12.9 %copy-start.2 = (bf16[128,64]{0,1:T(8,128)(2,1)S(1)}, bf16[128,64]{0,1:T(8,128)(2,1)}, u32[]{:S(2)}) copy-start(bf16[128,64]{0,1:T(8,128)(2,1)} %param.9) | copy-start | bytes 49156
  0.7 12.9 %copy-start.3 = (s32[128,2]{0,1:T(2,128)S(1)}, s32[128,2]{0,1:T(2,128)}, u32[]{:S(2)}) copy-start(s32[128,2]{0,1:T(2,128)} %param.10) | copy-start | bytes 3076
  0.7 12.9 %copy-start.4 = (f32[128,2]{0,1:T(2,128)S(1)}, f32[128,2]{0,1:T(2,128)}, u32[]{:S(2)}) copy-start(f32[128,2]{0,1:T(2,128)} %param.11) | copy-start | bytes 3076
  0.7 27.9 %copy-start.5 = (f32[1536]{0:T(1024)S(1)}, f32[1536]{0:T(1024)}, u32[]{:S(2)}) copy-start(f32[1536]{0:T(1024)} %param.12) | copy-start | bytes 18436
  0.7 27.9 %copy-start.6 = (f32[1536]{0:T(1024)S(1)}, f32[1536]{0:T(1024)}, u32[]{:S(2)}) copy-start(f32[1536]{0:T(1024)} %param.13) | copy-start | bytes 18436
  2.0 42.5 %collective-permute-start = (bf16[384,1536]{1,0:T(8,128)(2,1)S(1)}, bf16[384,1536]{1,0:T(8,128)(2,1)S(1)}, u32[]{:S(2)}, u32[]{:S(2)}) collective-permute-start(bf16[384,1536]{1,0:T(8,128)(2,1)S(1)} %pad_maximum_fusion.w0), channel_id=1, source_target_pairs={{0,48},{48,0},{1,49},{49,1},{2,50},{50,2},{3,51},{51,3},{4,52},{52... | collective-permute-start | bytes 3538952 | tf_op jit(solution)/shard_map/ppermute | solution.py:237
  14.6 30.0 %all-to-all-start = ((bf16[48,16,128]{2,1,0:T(8,128)(2,1)}), bf16[48,16,128]{2,1,0:T(8,128)(2,1)S(1)}, u32[]{:S(2)}, u32[]{:S(2)}) async-start(bf16[48,16,128]{2,1,0:T(8,128)(2,1)} %bitcast.4), calls=%async_computation | async-start | bytes 393216 | tf_op jit(solution)/shard_map/all_to_all | solution.py:233
  26.7 24.9 %collective-permute-start.1 = (bf16[384,1536]{1,0:T(8,128)(2,1)S(1)}, bf16[384,1536]{1,0:T(8,128)(2,1)}, u32[]{:S(2)}, u32[]{:S(2)}) collective-permute-start(bf16[384,1536]{1,0:T(8,128)(2,1)S(1)} %pad_maximum_fusion.w0), channel_id=1, source_target_pairs={{0,24},{24,0},{1,25},{25,1},{2,26},{26,2},{3,27},{27,3},{4,28},{28... | collective-permute-start | bytes 3538952 | tf_op jit(solution)/shard_map/ppermute | solution.py:238
  44.9 0.9 copy-start
  45.8 13.5 %all-to-all-start.1 = ((bf16[4,64,1536]{2,1,0:T(8,128)(2,1)}), bf16[4,64,1536]{2,1,0:T(8,128)(2,1)S(1)}, u32[]{:S(2)}, u32[]{:S(2)}) async-start(bf16[4,64,1536]{2,1,0:T(8,128)(2,1)} %copy-done), calls=%async_computation.1 | async-start | bytes 1572864 | tf_op jit(solution)/shard_map/all_to_all | solution.py:249
  49.6 9.7 %collective-permute-start.2 = (bf16[384,1536]{1,0:T(8,128)(2,1)S(1)}, bf16[384,1536]{1,0:T(8,128)(2,1)}, u32[]{:S(2)}, u32[]{:S(2)}) collective-permute-start(bf16[384,1536]{1,0:T(8,128)(2,1)S(1)} %collective-permute-done.w1), channel_id=1, source_target_pairs={{0,24},{24,0},{1,25},{25,1},{2,26},{26,2},{3,27},{27,3},{4,28},{28... | collective-permute-start | bytes 3538952 | tf_op jit(solution)/shard_map/ppermute | solution.py:241
  63.0 18.1 %collective-permute-start.3 = (bf16[768,1536]{1,0:T(8,128)(2,1)S(1)}, bf16[768,1536]{1,0:T(8,128)(2,1)S(1)}, u32[]{:S(2)}, u32[]{:S(2)}) collective-permute-start(bf16[768,1536]{1,0:T(8,128)(2,1)S(1)} %shard_map.114), channel_id=1, source_target_pairs={{0,24},{24,0},{1,25},{25,1},{2,26},{26,2},{3,27},{27,3},{4,28},{28... | collective-permute-start | bytes 7077896 | tf_op jit(solution)/shard_map/ppermute | solution.py:272
  81.6 31.6 %collective-permute-start.4 = (bf16[384,1536]{1,0:T(8,128)(2,1)S(1)}, bf16[384,1536]{1,0:T(8,128)(2,1)S(1)}, u32[]{:S(2)}, u32[]{:S(2)}) collective-permute-start(bf16[384,1536]{1,0:T(8,128)(2,1)S(1)} %shard_map.117), channel_id=1, source_target_pairs={{0,48},{48,0},{1,49},{49,1},{2,50},{50,2},{3,51},{51,3},{4,52},{52... | collective-permute-start | bytes 3538952 | tf_op jit(solution)/shard_map/ppermute | solution.py:281

commit v3 on v2

--- a/solution.py
+++ b/solution.py
@@ -15,9 +15,11 @@
 SLOTS = EXPERTS * CAP
 ROWS = Y_FAR * CAP
 GROUP = Y_NEAR * X_HI
+PARTNERS = (("ynear", "xhi"), ("xhi",), ("ynear",))
 DP_AXES = ("yfar", "ynear", "xhi", "xlo", "core")
 EXPERT_AXES = ("yh", "z")
 SWAP = [(0, 1), (1, 0)]
+SWAP_BOTH = [(0, 3), (1, 2), (2, 1), (3, 0)]
 MIB = 1024 * 1024
 F32 = jnp.float32
 VMEM, ANY = pltpu.VMEM, pl.ANY
@@ -112,10 +114,15 @@
 
 
 def gathered(x, first):
-    return jnp.concatenate([x[g, first : first + ROWS] for g in range(GROUP)], axis=0)
-
-
-def expert_kernel(x, w0, w1, w2, w3, part_ref, hid_ref, back_ref, v2, v3, sems):
+    near, high = lax.axis_index("ynear"), lax.axis_index("xhi")
+    order = [near * X_HI + high]
+    for flips in PARTNERS:
+        y = 1 - near if "ynear" in flips else near
+        order.append(y * X_HI + (1 - high if "xhi" in flips else high))
+    return jnp.concatenate([x[i, first : first + ROWS] for i in order], axis=0)
+
+
+def expert_kernel(x, w0, w1, w2, w3, p0, p1, p2, p3, hid_ref, back_ref, v2, v3, sems):
     width = x.shape[2]
     units = w0.shape[0] // 2
     loads = [
@@ -139,10 +146,10 @@
         back_ref[i] = back_inner
         forward += dot(hidden, weight_out, 1, 0)
         backward += dot(back_inner, weight_in, 1, 0)
-    for g in range(GROUP):
-        rows = slice(g * ROWS, (g + 1) * ROWS)
-        part_ref[g, :, :width] = forward[rows].astype(BF16)
-        part_ref[g, :, width:] = backward[rows].astype(BF16)
+    for i, p in enumerate((p0, p1, p2, p3)):
+        rows = slice(i * ROWS, (i + 1) * ROWS)
+        p[:, :width] = forward[rows].astype(p.dtype)
+        p[:, width:] = backward[rows].astype(p.dtype)
 
 
 def grad_pair(x, hid_ref, back_ref, i):
@@ -183,11 +190,11 @@
         copy.wait()
 
 
-def back_kernel(part_ref, rows_ref, gain_ref, out_ref):
+def back_kernel(p0, p1, p2, p3, rows_ref, gain_ref, out_ref):
     width = rows_ref.shape[1]
 
     def total(cols):
-        parts = [part_ref[g, :, cols].astype(F32) for g in range(GROUP)]
+        parts = [p[:, cols].astype(F32) for p in (p0, p1, p2, p3)]
         return (parts[0] + parts[1]) + (parts[2] + parts[3])
 
     unit, scaled = normal(rows_ref[...].astype(F32))
@@ -237,7 +244,6 @@
     w1 = lax.ppermute(w0, "xlo", SWAP)
     w2 = lax.ppermute(w0, "core", SWAP)
     came = exchange(call(route_kernel, blocks)(routes_t, gates_t, frames_t, cotangent_t))
-    came, w1 = lax.optimization_barrier((came, w1))
     w3 = lax.ppermute(w1, "core", SWAP)
     spread, rows = call(
         normalize_kernel,
@@ -245,23 +251,24 @@
         scratch_shapes=[VMEM((ROWS, width), F32)],
     )(came, gain, bias)
 
-    def group(a):
-        return lax.all_to_all(a, ("ynear", "xhi"), split_axis=0, concat_axis=0, tiled=True)
-
-    x = group(spread)
+    x = lax.all_to_all(spread, ("ynear", "xhi"), split_axis=0, concat_axis=0, tiled=True)
     kept = shape((4, GROUP * ROWS, units), BF16)
     stack = (2 * units, width)
     work = 4 * GROUP * ROWS * units * width
-    parts, hidden, back_inner = call(
+    part = shape((ROWS, 2 * width), BF16)
+    p0, *parts, hidden, back_inner = call(
         expert_kernel,
-        (shape((GROUP, ROWS, 2 * width), BF16), kept, kept),
+        (shape((ROWS, 2 * width), F32), part, part, part, kept, kept),
         flops=8 * work,
         bytes_accessed=16 * units * width,
         vmem=16,
         in_specs=spaces(VMEM, VMEM, VMEM, ANY, ANY),
         scratch_shapes=[VMEM(stack, BF16), VMEM(stack, BF16), DMA((2,))],
     )(x, w0, w1, w2, w3)
-    came_parts = group(parts)
+    came_parts = [
+        lax.ppermute(p, flips, SWAP_BOTH if len(flips) == 2 else SWAP)
+        for p, flips in zip(parts, PARTNERS)
+    ]
     for_sib = call(
         grads_kernel,
         shape((4 * units, width), BF16),
@@ -270,11 +277,10 @@
         vmem=12,
     )(x, hidden, back_inner)
     from_sib = lax.ppermute(for_sib, "core", SWAP)
-    came_parts, from_sib = lax.optimization_barrier((came_parts, from_sib))
     for_far = call(
         fold_kernel,
         shape(stack, BF16),
-        flops=work,
+        flops=100000000000,
         bytes_accessed=8 * units * width,
         vmem=12,
     )(x, hidden, back_inner, from_sib)
@@ -289,7 +295,7 @@
         out_specs=spaces(ANY, ANY),
         scratch_shapes=[VMEM((units, width), F32), VMEM((units, width), F32), DMA((2,))],
     )(x, hidden, back_inner, from_sib, from_far)
-    backs = exchange(call(back_kernel, blocks)(came_parts, rows, gain))
+    backs = exchange(call(back_kernel, blocks, flops=100000000000)(p0, *came_parts, rows, gain))
     token = shape(frames_t.shape, BF16)
     output, frame_grads = call(combine_kernel, (token, token))(
         backs, routes_t, gates_t, frames_t, cotangent_t

time: 115 us -> 109 us (0.948)
  the two profiles are of different devices: /device:TPU:2 before, /device:TPU:8 now
where the time goes in v3:
time: 109 us
  starting transfers between devices  47.6 us (44%)
  waiting for transfers between devices  25.8 us (24%)
  blocking collectives  23.7 us (22%)
  Pallas kernels  8.71 us (8%)
  other arithmetic  1.35 us (1%)
    all_to_all x1, blocking collectives, exchange(): lax.all_to_all(a, ('yfar',) + EXPERT_AXES, split_axis=0, concat_axis=0, t...  23.7 us
    all_to_all x1, starting transfers between devices, exchange(): lax.all_to_all(a, ('yfar',) + EXPERT_AXES, split_axis=0, concat_axis=0, t...  20.2 us
    all_to_all x1, waiting for transfers between devices, exchange(): lax.all_to_all(a, ('yfar',) + EXPERT_AXES, split_axis=0, concat_axis=0, t...  16 us
    ppermute x3, starting transfers between devices, body(): lax.ppermute(p, flips, SWAP_BOTH if len(flips) == 2 else SWAP)  10.7 us
    all_to_all x1, waiting for transfers between devices, body(): lax.all_to_all(spread, ('ynear', 'xhi'), split_axis=0, concat_axis=0, til...  7.18 us
    all_to_all x1, starting transfers between devices, body(): lax.all_to_all(spread, ('ynear', 'xhi'), split_axis=0, concat_axis=0, til...  5.46 us
    ppermute x1, starting transfers between devices, body(): w1 = lax.ppermute(w0, 'xlo', SWAP)  3.4 us
    pallas_call x1, Pallas kernels, body(): call(expert_kernel, (shape((ROWS, 2 * width), F32), part, part, part, kep...  2.94 us
  transfers between devices with their start and end apart: 10, of which 4 were waited for; matrix products, arithmetic and copies ran while one was open for 0% of the time, Pallas kernels for 3%

profile of v3, /device:TPU:8, one launch (start us, length us, event | category | flops | bytes accessed | tf_op | source)
XLA Modules:
  0.0 108.9 jit_solution(8360878469687976188)
XLA Ops:
  0.6 0.0 copy-start.1
  0.6 0.0 copy-start.3
  0.7 0.0 copy-start.5
  0.7 0.0 copy-start.7
  0.7 0.0 copy-start.9
  0.7 0.0 copy-start.10
  0.7 1.3 %pad_maximum_fusion.w0 = bf16[384,1536]{1,0:T(8,128)(2,1)S(1)} fusion(bf16[192,1536]{1,0:T(8,128)(2,1)} %bitcast.29, bf16[192,1536]{1,0:T(8,128)(2,1)} %bitcast.30), kind=kLoop, calls=%fused_computation | loop fusion | flops 2359296 | bytes 2359296 | tf_op jit(solution)/shard_map/concatenate | solution.py:243
  2.1 3.4 %collective-permute-start = (bf16[384,1536]{1,0:T(8,128)(2,1)S(1)}, bf16[384,1536]{1,0:T(8,128)(2,1)S(1)}, u32[]{:S(2)}, u32[]{:S(2)}) collective-permute-start(bf16[384,1536]{1,0:T(8,128)(2,1)S(1)} %pad_maximum_fusion.w0), channel_id=1, source_target_pairs={{0,48},{48,0},{1,49},{49,1},{2,50},{50,2},{3,51},{51,3},{4,52},{52... | collective-permute-start | bytes 3538952 | tf_op jit(solution)/shard_map/ppermute | solution.py:244
  5.5 0.0 copy-done.1
  5.5 0.0 copy-done.3
  5.5 0.0 copy-done.5
  5.5 0.0 copy-done.7
  5.5 1.0 shard_map.111
  6.5 20.2 %all-to-all-start = ((bf16[48,16,128]{2,1,0:T(8,128)(2,1)}), bf16[48,16,128]{2,1,0:T(8,128)(2,1)S(1)}, u32[]{:S(2)}, u32[]{:S(2)}) async-start(bf16[48,16,128]{2,1,0:T(8,128)(2,1)} %bitcast.4), calls=%async_computation | async-start | bytes 393216 | tf_op jit(solution)/shard_map/all_to_all | solution.py:240
  26.7 1.9 %collective-permute-start.1 = (bf16[384,1536]{1,0:T(8,128)(2,1)S(1)}, bf16[384,1536]{1,0:T(8,128)(2,1)}, u32[]{:S(2)}, u32[]{:S(2)}) collective-permute-start(bf16[384,1536]{1,0:T(8,128)(2,1)S(1)} %pad_maximum_fusion.w0), channel_id=1, source_target_pairs={{0,24},{24,0},{1,25},{25,1},{2,26},{26,2},{3,27},{27,3},{4,28},{28... | collective-permute-start | bytes 3538952 | tf_op jit(solution)/shard_map/ppermute | solution.py:245
  28.6 0.0 copy-done.9
  28.7 0.0 copy-done.10
  28.7 16.0 %all-to-all-done = bf16[48,16,128]{2,1,0:T(8,128)(2,1)S(1)} async-done(((bf16[48,16,128]{2,1,0:T(8,128)(2,1)}), bf16[48,16,128]{2,1,0:T(8,128)(2,1)S(1)}, u32[]{:S(2)}, u32[]{:S(2)}) %all-to-all-start) | async-done | bytes 196640 | tf_op jit(solution)/shard_map/all_to_all | solution.py:240
  44.7 0.3 shard_map.112
  45.0 0.0 copy-start
  45.0 0.9 copy-done
  45.9 5.5 %all-to-all-start.1 = ((bf16[4,64,1536]{2,1,0:T(8,128)(2,1)}), bf16[4,64,1536]{2,1,0:T(8,128)(2,1)S(1)}, u32[]{:S(2)}, u32[]{:S(2)}) async-start(bf16[4,64,1536]{2,1,0:T(8,128)(2,1)} %copy-done), calls=%async_computation.1 | async-start | bytes 1572864 | tf_op jit(solution)/shard_map/all_to_all | solution.py:254
  51.3 0.0 collective-permute-done.w1
  51.3 1.9 %collective-permute-start.2 = (bf16[384,1536]{1,0:T(8,128)(2,1)S(1)}, bf16[384,1536]{1,0:T(8,128)(2,1)}, u32[]{:S(2)}, u32[]{:S(2)}) collective-permute-start(bf16[384,1536]{1,0:T(8,128)(2,1)S(1)} %collective-permute-done.w1), channel_id=1, source_target_pairs={{0,24},{24,0},{1,25},{25,1},{2,26},{26,2},{3,27},{27,3},{4,28},{28... | collective-permute-start | bytes 3538952 | tf_op jit(solution)/shard_map/ppermute | solution.py:247
  53.2 0.0 collective-permute-done.1.w2
  53.2 7.2 %all-to-all-done.1.x = bf16[4,64,1536]{2,1,0:T(8,128)(2,1)S(1)} async-done(((bf16[4,64,1536]{2,1,0:T(8,128)(2,1)}), bf16[4,64,1536]{2,1,0:T(8,128)(2,1)S(1)}, u32[]{:S(2)}, u32[]{:S(2)}) %all-to-all-start.1) | async-done | bytes 786464 | tf_op jit(solution)/shard_map/all_to_all | solution.py:254
  60.4 0.0 collective-permute-done.2.w3
  60.4 2.9 %shard_map.113 = (f32[32,3072]{1,0:T(8,128)S(1)}, bf16[32,3072]{1,0:T(8,128)(2,1)S(1)}, bf16[32,3072]{1,0:T(8,128)(2,1)S(1)}, bf16[32,3072]{1,0:T(8,128)(2,1)S(1...) custom-call(bf16[4,64,1536]{2,1,0:T(8,128)(2,1)S(1)} %all-to-all-done.1.x, ...), custom_call_target="tpu_custom_call" | custom-call | flops 1207959552 | bytes 4718592 | tf_op jit(solution)/shard_map/pallas_call | solution.py:259
  63.4 0.8 shard_map.116
  64.2 1.9 %collective-permute-start.6 = (bf16[768,1536]{1,0:T(8,128)(2,1)S(1)}, bf16[768,1536]{1,0:T(8,128)(2,1)S(1)}, u32[]{:S(2)}, u32[]{:S(2)}) collective-permute-start(bf16[768,1536]{1,0:T(8,128)(2,1)S(1)} %shard_map.116), channel_id=1, source_target_pairs={{0,24},{24,0},{1,25},{25,1},{2,26},{26,2},{3,27},{27,3},{4,28},{28... | collective-permute-start | bytes 7077896 | tf_op jit(solution)/shard_map/ppermute | solution.py:279
  66.1 3.5 %collective-permute-start.3 = (bf16[32,3072]{1,0:T(8,128)(2,1)S(1)}, bf16[32,3072]{1,0:T(8,128)(2,1)S(1)}, u32[]{:S(2)}, u32[]{:S(2)}) collective-permute-start(bf16[32,3072]{1,0:T(8,128)(2,1)S(1)} %get-tuple-element.18), channel_id=1, source_target_pairs={{0,288},{96,192},{192,96},{288,0},{1,289},{97,193},{193,97},{289,1... | collective-permute-start | bytes 589832 | tf_op jit(solution)/shard_map/ppermute | solution.py:269
  69.6 3.9 %collective-permute-start.4 = (bf16[32,3072]{1,0:T(8,128)(2,1)S(1)}, bf16[32,3072]{1,0:T(8,128)(2,1)S(1)}, u32[]{:S(2)}, u32[]{:S(2)}) collective-permute-start(bf16[32,3072]{1,0:T(8,128)(2,1)S(1)} %get-tuple-element.19), channel_id=1, source_target_pairs={{0,96},{96,0},{1,97},{97,1},{2,98},{98,2},{3,99},{99,3},{4,100},{1... | collective-permute-start | bytes 589832 | tf_op jit(solution)/shard_map/ppermute | solution.py:269
  73.4 3.4 %collective-permute-start.5 = (bf16[32,3072]{1,0:T(8,128)(2,1)S(1)}, bf16[32,3072]{1,0:T(8,128)(2,1)S(1)}, u32[]{:S(2)}, u32[]{:S(2)}) collective-permute-start(bf16[32,3072]{1,0:T(8,128)(2,1)S(1)} %get-tuple-element.20), channel_id=1, source_target_pairs={{0,192},{192,0},{1,193},{193,1},{2,194},{194,2},{3,195},{195,3},{4... | collective-permute-start | bytes 589832 | tf_op jit(solution)/shard_map/ppermute | solution.py:269
  76.8 0.0 collective-permute-done.6.came_ref
  76.9 0.5 shard_map.117
  77.3 2.1 %collective-permute-start.7 = (bf16[384,1536]{1,0:T(8,128)(2,1)S(1)}, bf16[384,1536]{1,0:T(8,128)(2,1)S(1)}, u32[]{:S(2)}, u32[]{:S(2)}) collective-permute-start(bf16[384,1536]{1,0:T(8,128)(2,1)S(1)} %shard_map.117), channel_id=1, source_target_pairs={{0,48},{48,0},{1,49},{49,1},{2,50},{50,2},{3,51},{51,3},{4,52},{52... | collective-permute-start | bytes 3538952 | tf_op jit(solution)/shard_map/ppermute | solution.py:287
  79.5 0.0 collective-permute-done.3.p1
  79.5 2.5 %collective-permute-done.4.p2 = bf16[32,3072]{1,0:T(8,128)(2,1)S(1)} collective-permute-done((bf16[32,3072]{1,0:T(8,128)(2,1)S(1)}, bf16[32,3072]{1,0:T(8,128)(2,1)S(1)}, u32[]{:S(2)}, u32[]{:S(2)}) %collective-permute-start.4) | collective-permute-done | bytes 196640 | tf_op jit(solution)/shard_map/ppermute | solution.py:269
  82.0 0.1 collective-permute-done.5.p3
  82.1 0.0 copy-start.2
  82.1 0.0 copy-start.4
  82.1 0.0 copy-start.6
  82.1 0.0 copy-start.8
  82.1 0.4 shard_map.114
  82.5 23.7 %all_to_all.15 = bf16[48,16,128]{2,1,0:T(8,128)(2,1)S(1)} all-to-all(bf16[48,16,128]{2,1,0:T(8,128)(2,1)S(1)} %bitcast.20), channel_id=1, replica_groups=mesh['yfar'=2,'ynear'=2,'xhi'=2,'xlo'=2,'core'=2,'yh'=2,'z'=12] {'yfar',..., dimensions={0} | all-to-all | bytes 393216 | tf_op jit(solution)/shard_map/all_to_all | solution.py:240
  106.2 0.0 copy-done.2
  106.2 0.0 copy-done.4
  106.2 0.0 copy-done.6
  106.2 0.0 copy-done.8
  106.2 1.0 shard_map.115
  107.2 0.0 collective-permute-done.7.far_ref
  107.2 1.8 %shard_map.118 = (f32[192,1536]{1,0:T(8,128)}, f32[192,1536]{1,0:T(8,128)}) custom-call(bf16[4,64,1536]{2,1,0:T(8,128)(2,1)S(1)} %all-to-all-done.1.x, bf16[4,128,192]{2,1,0:T(8,128)(2,1)S(1)} %get-tuple-element.24.hid_ref, bf16[4,128,192]{2,1,0:T(8,128)(2,1)S(1)} %get-tuple-element.25.back_ref, bf16[768,1536]{1,0:T(8,128)(2,1)S(1)} %collective-permute-done.6.came_ref, ...), custom_call_target="tpu_custom_call" | custom-call | flops 150994944 | bytes 4718592 | tf_op jit(solution)/shard_map/pallas_call | solution.py:289
  (2 shorter events, 0.0 us)
Async XLA Ops:
  0.6 4.8 %copy-start.1 = (bf16[128,64]{0,1:T(8,128)(2,1)S(1)}, bf16[128,64]{0,1:T(8,128)(2,1)}, u32[]{:S(2)}) copy-start(bf16[128,64]{0,1:T(8,128)(2,1)} %param.8) | copy-start | bytes 49156
  0.6 4.8 %copy-start.3 = (bf16[128,64]{0,1:T(8,128)(2,1)S(1)}, bf16[128,64]{0,1:T(8,128)(2,1)}, u32[]{:S(2)}) copy-start(bf16[128,64]{0,1:T(8,128)(2,1)} %param.9) | copy-start | bytes 49156
  0.7 4.8 %copy-start.5 = (s32[128,2]{0,1:T(2,128)S(1)}, s32[128,2]{0,1:T(2,128)}, u32[]{:S(2)}) copy-start(s32[128,2]{0,1:T(2,128)} %param.10) | copy-start | bytes 3076
  0.7 4.8 %copy-start.7 = (f32[128,2]{0,1:T(2,128)S(1)}, f32[128,2]{0,1:T(2,128)}, u32[]{:S(2)}) copy-start(f32[128,2]{0,1:T(2,128)} %param.11) | copy-start | bytes 3076
  0.7 28.0 %copy-start.9 = (f32[1536]{0:T(1024)S(1)}, f32[1536]{0:T(1024)}, u32[]{:S(2)}) copy-start(f32[1536]{0:T(1024)} %param.12) | copy-start | bytes 18436
  0.7 28.0 %copy-start.10 = (f32[1536]{0:T(1024)S(1)}, f32[1536]{0:T(1024)}, u32[]{:S(2)}) copy-start(f32[1536]{0:T(1024)} %param.13) | copy-start | bytes 18436
  2.1 49.3 %collective-permute-start = (bf16[384,1536]{1,0:T(8,128)(2,1)S(1)}, bf16[384,1536]{1,0:T(8,128)(2,1)S(1)}, u32[]{:S(2)}, u32[]{:S(2)}) collective-permute-start(bf16[384,1536]{1,0:T(8,128)(2,1)S(1)} %pad_maximum_fusion.w0), channel_id=1, source_target_pairs={{0,48},{48,0},{1,49},{49,1},{2,50},{50,2},{3,51},{51,3},{4,52},{52... | collective-permute-start | bytes 3538952 | tf_op jit(solution)/shard_map/ppermute | solution.py:244
  6.5 38.1 %all-to-all-start = ((bf16[48,16,128]{2,1,0:T(8,128)(2,1)}), bf16[48,16,128]{2,1,0:T(8,128)(2,1)S(1)}, u32[]{:S(2)}, u32[]{:S(2)}) async-start(bf16[48,16,128]{2,1,0:T(8,128)(2,1)} %bitcast.4), calls=%async_computation | async-start | bytes 393216 | tf_op jit(solution)/shard_map/all_to_all | solution.py:240
  26.7 26.5 %collective-permute-start.1 = (bf16[384,1536]{1,0:T(8,128)(2,1)S(1)}, bf16[384,1536]{1,0:T(8,128)(2,1)}, u32[]{:S(2)}, u32[]{:S(2)}) collective-permute-start(bf16[384,1536]{1,0:T(8,128)(2,1)S(1)} %pad_maximum_fusion.w0), channel_id=1, source_target_pairs={{0,24},{24,0},{1,25},{25,1},{2,26},{26,2},{3,27},{27,3},{4,28},{28... | collective-permute-start | bytes 3538952 | tf_op jit(solution)/shard_map/ppermute | solution.py:245
  45.0 0.9 copy-start
  45.9 14.6 %all-to-all-start.1 = ((bf16[4,64,1536]{2,1,0:T(8,128)(2,1)}), bf16[4,64,1536]{2,1,0:T(8,128)(2,1)S(1)}, u32[]{:S(2)}, u32[]{:S(2)}) async-start(bf16[4,64,1536]{2,1,0:T(8,128)(2,1)} %copy-done), calls=%async_computation.1 | async-start | bytes 1572864 | tf_op jit(solution)/shard_map/all_to_all | solution.py:254
  51.3 9.1 %collective-permute-start.2 = (bf16[384,1536]{1,0:T(8,128)(2,1)S(1)}, bf16[384,1536]{1,0:T(8,128)(2,1)}, u32[]{:S(2)}, u32[]{:S(2)}) collective-permute-start(bf16[384,1536]{1,0:T(8,128)(2,1)S(1)} %collective-permute-done.w1), channel_id=1, source_target_pairs={{0,24},{24,0},{1,25},{25,1},{2,26},{26,2},{3,27},{27,3},{4,28},{28... | collective-permute-start | bytes 3538952 | tf_op jit(solution)/shard_map/ppermute | solution.py:247
  64.2 12.7 %collective-permute-start.6 = (bf16[768,1536]{1,0:T(8,128)(2,1)S(1)}, bf16[768,1536]{1,0:T(8,128)(2,1)S(1)}, u32[]{:S(2)}, u32[]{:S(2)}) collective-permute-start(bf16[768,1536]{1,0:T(8,128)(2,1)S(1)} %shard_map.116), channel_id=1, source_target_pairs={{0,24},{24,0},{1,25},{25,1},{2,26},{26,2},{3,27},{27,3},{4,28},{28... | collective-permute-start | bytes 7077896 | tf_op jit(solution)/shard_map/ppermute | solution.py:279
  66.1 13.4 %collective-permute-start.3 = (bf16[32,3072]{1,0:T(8,128)(2,1)S(1)}, bf16[32,3072]{1,0:T(8,128)(2,1)S(1)}, u32[]{:S(2)}, u32[]{:S(2)}) collective-permute-start(bf16[32,3072]{1,0:T(8,128)(2,1)S(1)} %get-tuple-element.18), channel_id=1, source_target_pairs={{0,288},{96,192},{192,96},{288,0},{1,289},{97,193},{193,97},{289,1... | collective-permute-start | bytes 589832 | tf_op jit(solution)/shard_map/ppermute | solution.py:269
  69.6 12.4 %collective-permute-start.4 = (bf16[32,3072]{1,0:T(8,128)(2,1)S(1)}, bf16[32,3072]{1,0:T(8,128)(2,1)S(1)}, u32[]{:S(2)}, u32[]{:S(2)}) collective-permute-start(bf16[32,3072]{1,0:T(8,128)(2,1)S(1)} %get-tuple-element.19), channel_id=1, source_target_pairs={{0,96},{96,0},{1,97},{97,1},{2,98},{98,2},{3,99},{99,3},{4,100},{1... | collective-permute-start | bytes 589832 | tf_op jit(solution)/shard_map/ppermute | solution.py:269
  73.4 8.6 %collective-permute-start.5 = (bf16[32,3072]{1,0:T(8,128)(2,1)S(1)}, bf16[32,3072]{1,0:T(8,128)(2,1)S(1)}, u32[]{:S(2)}, u32[]{:S(2)}) collective-permute-start(bf16[32,3072]{1,0:T(8,128)(2,1)S(1)} %get-tuple-element.20), channel_id=1, source_target_pairs={{0,192},{192,0},{1,193},{193,1},{2,194},{194,2},{3,195},{195,3},{4... | collective-permute-start | bytes 589832 | tf_op jit(solution)/shard_map/ppermute | solution.py:269
  77.3 29.8 %collective-permute-start.7 = (bf16[384,1536]{1,0:T(8,128)(2,1)S(1)}, bf16[384,1536]{1,0:T(8,128)(2,1)S(1)}, u32[]{:S(2)}, u32[]{:S(2)}) collective-permute-start(bf16[384,1536]{1,0:T(8,128)(2,1)S(1)} %shard_map.117), channel_id=1, source_target_pairs={{0,48},{48,0},{1,49},{49,1},{2,50},{50,2},{3,51},{51,3},{4,52},{52... | collective-permute-start | bytes 3538952 | tf_op jit(solution)/shard_map/ppermute | solution.py:287
  82.1 24.1 %copy-start.2 = (bf16[128,64]{0,1:T(8,128)(2,1)S(1)}, bf16[128,64]{0,1:T(8,128)(2,1)}, u32[]{:S(2)}) copy-start(bf16[128,64]{0,1:T(8,128)(2,1)} %param.8) | copy-start | bytes 49156
  82.1 24.1 %copy-start.4 = (bf16[128,64]{0,1:T(8,128)(2,1)S(1)}, bf16[128,64]{0,1:T(8,128)(2,1)}, u32[]{:S(2)}) copy-start(bf16[128,64]{0,1:T(8,128)(2,1)} %param.9) | copy-start | bytes 49156
  82.1 24.1 %copy-start.6 = (s32[128,2]{0,1:T(2,128)S(1)}, s32[128,2]{0,1:T(2,128)}, u32[]{:S(2)}) copy-start(s32[128,2]{0,1:T(2,128)} %param.10) | copy-start | bytes 3076
  82.1 24.1 %copy-start.8 = (f32[128,2]{0,1:T(2,128)S(1)}, f32[128,2]{0,1:T(2,128)}, u32[]{:S(2)}) copy-start(f32[128,2]{0,1:T(2,128)} %param.11) | copy-start | bytes 3076

commit v4 on v3

--- a/solution.py
+++ b/solution.py
@@ -14,8 +14,8 @@
 CAP = 16
 SLOTS = EXPERTS * CAP
 ROWS = Y_FAR * CAP
-GROUP = Y_NEAR * X_HI
-PARTNERS = (("ynear", "xhi"), ("xhi",), ("ynear",))
+GROUP = Y_NEAR * X_LO
+PARTNERS = (("ynear", "xlo"), ("xlo",), ("ynear",))
 DP_AXES = ("yfar", "ynear", "xhi", "xlo", "core")
 EXPERT_AXES = ("yh", "z")
 SWAP = [(0, 1), (1, 0)]
@@ -114,11 +114,11 @@
 
 
 def gathered(x, first):
-    near, high = lax.axis_index("ynear"), lax.axis_index("xhi")
-    order = [near * X_HI + high]
+    near, high = lax.axis_index("ynear"), lax.axis_index("xlo")
+    order = [near * X_LO + high]
     for flips in PARTNERS:
         y = 1 - near if "ynear" in flips else near
-        order.append(y * X_HI + (1 - high if "xhi" in flips else high))
+        order.append(y * X_LO + (1 - high if "xlo" in flips else high))
     return jnp.concatenate([x[i, first : first + ROWS] for i in order], axis=0)
 
 
@@ -241,7 +241,7 @@
         return a.reshape(Y_FAR, EXPERTS, CAP, LANES)
 
     w0 = jnp.concatenate([in_own, out_own], axis=0)
-    w1 = lax.ppermute(w0, "xlo", SWAP)
+    w1 = lax.ppermute(w0, "xhi", SWAP)
     w2 = lax.ppermute(w0, "core", SWAP)
     came = exchange(call(route_kernel, blocks)(routes_t, gates_t, frames_t, cotangent_t))
     w3 = lax.ppermute(w1, "core", SWAP)
@@ -251,7 +251,7 @@
         scratch_shapes=[VMEM((ROWS, width), F32)],
     )(came, gain, bias)
 
-    x = lax.all_to_all(spread, ("ynear", "xhi"), split_axis=0, concat_axis=0, tiled=True)
+    x = lax.all_to_all(spread, ("ynear", "xlo"), split_axis=0, concat_axis=0, tiled=True)
     kept = shape((4, GROUP * ROWS, units), BF16)
     stack = (2 * units, width)
     work = 4 * GROUP * ROWS * units * width
@@ -284,7 +284,7 @@
         bytes_accessed=8 * units * width,
         vmem=12,
     )(x, hidden, back_inner, from_sib)
-    from_far = lax.ppermute(for_far, "xlo", SWAP)
+    from_far = lax.ppermute(for_far, "xhi", SWAP)
     grad = shape((units, width), F32)
     grad_in, grad_out = call(
         finish_kernel,

time: 109 us -> 109 us (level)
  the two profiles are of different devices: /device:TPU:8 before, /device:TPU:2 now
where the time goes in v4:
time: 109 us; the launch traced here: 108 us
  starting transfers between devices  46.9 us (43%)
  waiting for transfers between devices  26 us (24%)
  blocking collectives  23.6 us (22%)
  Pallas kernels  8.7 us (8%)
  other arithmetic  1.35 us (1%)
    all_to_all x1, blocking collectives, exchange(): lax.all_to_all(a, ('yfar',) + EXPERT_AXES, split_axis=0, concat_axis=0, t...  23.6 us
    all_to_all x1, starting transfers between devices, exchange(): lax.all_to_all(a, ('yfar',) + EXPERT_AXES, split_axis=0, concat_axis=0, t...  21.1 us
    all_to_all x1, waiting for transfers between devices, exchange(): lax.all_to_all(a, ('yfar',) + EXPERT_AXES, split_axis=0, concat_axis=0, t...  15.9 us
    ppermute x3, starting transfers between devices, body(): lax.ppermute(p, flips, SWAP_BOTH if len(flips) == 2 else SWAP)  9.21 us
    all_to_all x1, waiting for transfers between devices, body(): lax.all_to_all(spread, ('ynear', 'xlo'), split_axis=0, concat_axis=0, til...  6.05 us
    all_to_all x1, starting transfers between devices, body(): lax.all_to_all(spread, ('ynear', 'xlo'), split_axis=0, concat_axis=0, til...  4.89 us
    ppermute x1, starting transfers between devices, body(): w1 = lax.ppermute(w0, 'xhi', SWAP)  4.03 us
    pallas_call x1, Pallas kernels, body(): call(expert_kernel, (shape((ROWS, 2 * width), F32), part, part, part, kep...  2.94 us
  transfers between devices with their start and end apart: 10, of which 5 were waited for; matrix products, arithmetic and copies ran while one was open for 0% of the time, Pallas kernels for 3%

profile of v4, /device:TPU:2, one launch (start us, length us, event | category | flops | bytes accessed | tf_op | source)
XLA Modules:
  0.0 108.4 jit_solution(15948539832235255951)
XLA Ops:
  0.6 0.0 copy-start.1
  0.6 0.0 copy-start.3
  0.7 0.0 copy-start.5
  0.7 0.0 copy-start.7
  0.7 0.0 copy-start.9
  0.7 0.0 copy-start.10
  0.7 1.3 %pad_maximum_fusion.w0 = bf16[384,1536]{1,0:T(8,128)(2,1)S(1)} fusion(bf16[192,1536]{1,0:T(8,128)(2,1)} %bitcast.29, bf16[192,1536]{1,0:T(8,128)(2,1)} %bitcast.30), kind=kLoop, calls=%fused_computation | loop fusion | flops 2359296 | bytes 2359296 | tf_op jit(solution)/shard_map/concatenate | solution.py:243
  2.1 4.0 %collective-permute-start = (bf16[384,1536]{1,0:T(8,128)(2,1)S(1)}, bf16[384,1536]{1,0:T(8,128)(2,1)S(1)}, u32[]{:S(2)}, u32[]{:S(2)}) collective-permute-start(bf16[384,1536]{1,0:T(8,128)(2,1)S(1)} %pad_maximum_fusion.w0), channel_id=1, source_target_pairs={{0,96},{96,0},{1,97},{97,1},{2,98},{98,2},{3,99},{99,3},{4,100},{1... | collective-permute-start | bytes 3538952 | tf_op jit(solution)/shard_map/ppermute | solution.py:244
  6.1 0.0 copy-done.1
  6.1 0.0 copy-done.3
  6.1 0.0 copy-done.5
  6.1 0.0 copy-done.7
  6.1 1.0 shard_map.111
  7.2 21.1 %all-to-all-start = ((bf16[48,16,128]{2,1,0:T(8,128)(2,1)}), bf16[48,16,128]{2,1,0:T(8,128)(2,1)S(1)}, u32[]{:S(2)}, u32[]{:S(2)}) async-start(bf16[48,16,128]{2,1,0:T(8,128)(2,1)} %bitcast.4), calls=%async_computation | async-start | bytes 393216 | tf_op jit(solution)/shard_map/all_to_all | solution.py:240
  28.2 1.9 %collective-permute-start.1 = (bf16[384,1536]{1,0:T(8,128)(2,1)S(1)}, bf16[384,1536]{1,0:T(8,128)(2,1)}, u32[]{:S(2)}, u32[]{:S(2)}) collective-permute-start(bf16[384,1536]{1,0:T(8,128)(2,1)S(1)} %pad_maximum_fusion.w0), channel_id=1, source_target_pairs={{0,24},{24,0},{1,25},{25,1},{2,26},{26,2},{3,27},{27,3},{4,28},{28... | collective-permute-start | bytes 3538952 | tf_op jit(solution)/shard_map/ppermute | solution.py:245
  30.2 0.0 copy-done.9
  30.2 0.0 copy-done.10
  30.2 15.9 %all-to-all-done = bf16[48,16,128]{2,1,0:T(8,128)(2,1)S(1)} async-done(((bf16[48,16,128]{2,1,0:T(8,128)(2,1)}), bf16[48,16,128]{2,1,0:T(8,128)(2,1)S(1)}, u32[]{:S(2)}, u32[]{:S(2)}) %all-to-all-start) | async-done | bytes 196640 | tf_op jit(solution)/shard_map/all_to_all | solution.py:240
  46.2 0.3 shard_map.112
  46.5 0.0 copy-start
  46.5 0.9 copy-done
  47.4 4.9 %all-to-all-start.1 = ((bf16[4,64,1536]{2,1,0:T(8,128)(2,1)}), bf16[4,64,1536]{2,1,0:T(8,128)(2,1)S(1)}, u32[]{:S(2)}, u32[]{:S(2)}) async-start(bf16[4,64,1536]{2,1,0:T(8,128)(2,1)} %copy-done), calls=%async_computation.1 | async-start | bytes 1572864 | tf_op jit(solution)/shard_map/all_to_all | solution.py:254
  52.3 0.0 collective-permute-done.w1
  52.3 1.9 %collective-permute-start.2 = (bf16[384,1536]{1,0:T(8,128)(2,1)S(1)}, bf16[384,1536]{1,0:T(8,128)(2,1)}, u32[]{:S(2)}, u32[]{:S(2)}) collective-permute-start(bf16[384,1536]{1,0:T(8,128)(2,1)S(1)} %collective-permute-done.w1), channel_id=1, source_target_pairs={{0,24},{24,0},{1,25},{25,1},{2,26},{26,2},{3,27},{27,3},{4,28},{28... | collective-permute-start | bytes 3538952 | tf_op jit(solution)/shard_map/ppermute | solution.py:247
  54.2 0.0 collective-permute-done.1.w2
  54.2 6.1 %all-to-all-done.1.x = bf16[4,64,1536]{2,1,0:T(8,128)(2,1)S(1)} async-done(((bf16[4,64,1536]{2,1,0:T(8,128)(2,1)}), bf16[4,64,1536]{2,1,0:T(8,128)(2,1)S(1)}, u32[]{:S(2)}, u32[]{:S(2)}) %all-to-all-start.1) | async-done | bytes 786464 | tf_op jit(solution)/shard_map/all_to_all | solution.py:254
  60.3 0.0 collective-permute-done.2.w3
  60.3 2.9 %shard_map.113 = (f32[32,3072]{1,0:T(8,128)S(1)}, bf16[32,3072]{1,0:T(8,128)(2,1)S(1)}, bf16[32,3072]{1,0:T(8,128)(2,1)S(1)}, bf16[32,3072]{1,0:T(8,128)(2,1)S(1...) custom-call(bf16[4,64,1536]{2,1,0:T(8,128)(2,1)S(1)} %all-to-all-done.1.x, ...), custom_call_target="tpu_custom_call" | custom-call | flops 1207959552 | bytes 4718592 | tf_op jit(solution)/shard_map/pallas_call | solution.py:259
  63.2 0.8 shard_map.116
  64.0 1.9 %collective-permute-start.6 = (bf16[768,1536]{1,0:T(8,128)(2,1)S(1)}, bf16[768,1536]{1,0:T(8,128)(2,1)S(1)}, u32[]{:S(2)}, u32[]{:S(2)}) collective-permute-start(bf16[768,1536]{1,0:T(8,128)(2,1)S(1)} %shard_map.116), channel_id=1, source_target_pairs={{0,24},{24,0},{1,25},{25,1},{2,26},{26,2},{3,27},{27,3},{4,28},{28... | collective-permute-start | bytes 7077896 | tf_op jit(solution)/shard_map/ppermute | solution.py:279
  65.9 3.3 %collective-permute-start.3 = (bf16[32,3072]{1,0:T(8,128)(2,1)S(1)}, bf16[32,3072]{1,0:T(8,128)(2,1)S(1)}, u32[]{:S(2)}, u32[]{:S(2)}) collective-permute-start(bf16[32,3072]{1,0:T(8,128)(2,1)S(1)} %get-tuple-element.18), channel_id=1, source_target_pairs={{0,240},{48,192},{192,48},{240,0},{1,241},{49,193},{193,49},{241,1... | collective-permute-start | bytes 589832 | tf_op jit(solution)/shard_map/ppermute | solution.py:269
  69.2 2.6 %collective-permute-start.4 = (bf16[32,3072]{1,0:T(8,128)(2,1)S(1)}, bf16[32,3072]{1,0:T(8,128)(2,1)S(1)}, u32[]{:S(2)}, u32[]{:S(2)}) collective-permute-start(bf16[32,3072]{1,0:T(8,128)(2,1)S(1)} %get-tuple-element.19), channel_id=1, source_target_pairs={{0,48},{48,0},{1,49},{49,1},{2,50},{50,2},{3,51},{51,3},{4,52},{52... | collective-permute-start | bytes 589832 | tf_op jit(solution)/shard_map/ppermute | solution.py:269
  71.8 3.4 %collective-permute-start.5 = (bf16[32,3072]{1,0:T(8,128)(2,1)S(1)}, bf16[32,3072]{1,0:T(8,128)(2,1)S(1)}, u32[]{:S(2)}, u32[]{:S(2)}) collective-permute-start(bf16[32,3072]{1,0:T(8,128)(2,1)S(1)} %get-tuple-element.20), channel_id=1, source_target_pairs={{0,192},{192,0},{1,193},{193,1},{2,194},{194,2},{3,195},{195,3},{4... | collective-permute-start | bytes 589832 | tf_op jit(solution)/shard_map/ppermute | solution.py:269
  75.2 0.0 collective-permute-done.6.came_ref
  75.2 0.5 shard_map.117
  75.7 1.9 %collective-permute-start.7 = (bf16[384,1536]{1,0:T(8,128)(2,1)S(1)}, bf16[384,1536]{1,0:T(8,128)(2,1)S(1)}, u32[]{:S(2)}, u32[]{:S(2)}) collective-permute-start(bf16[384,1536]{1,0:T(8,128)(2,1)S(1)} %shard_map.117), channel_id=1, source_target_pairs={{0,96},{96,0},{1,97},{97,1},{2,98},{98,2},{3,99},{99,3},{4,100},{1... | collective-permute-start | bytes 3538952 | tf_op jit(solution)/shard_map/ppermute | solution.py:287
  77.6 0.0 collective-permute-done.3.p1
  77.6 2.7 %collective-permute-done.4.p2 = bf16[32,3072]{1,0:T(8,128)(2,1)S(1)} collective-permute-done((bf16[32,3072]{1,0:T(8,128)(2,1)S(1)}, bf16[32,3072]{1,0:T(8,128)(2,1)S(1)}, u32[]{:S(2)}, u32[]{:S(2)}) %collective-permute-start.4) | collective-permute-done | bytes 196640 | tf_op jit(solution)/shard_map/ppermute | solution.py:269
  80.3 0.1 collective-permute-done.5.p3
  80.4 0.0 copy-start.2
  80.4 0.0 copy-start.4
  80.4 0.0 copy-start.6
  80.4 0.0 copy-start.8
  80.4 0.4 shard_map.114
  80.9 23.6 %all_to_all.15 = bf16[48,16,128]{2,1,0:T(8,128)(2,1)S(1)} all-to-all(bf16[48,16,128]{2,1,0:T(8,128)(2,1)S(1)} %bitcast.20), channel_id=1, replica_groups=mesh['yfar'=2,'ynear'=2,'xhi'=2,'xlo'=2,'core'=2,'yh'=2,'z'=12] {'yfar',..., dimensions={0} | all-to-all | bytes 393216 | tf_op jit(solution)/shard_map/all_to_all | solution.py:240
  104.5 0.0 copy-done.2
  104.5 0.0 copy-done.4
  104.5 0.0 copy-done.6
  104.5 0.0 copy-done.8
  104.5 1.0 shard_map.115
  105.5 1.1 %collective-permute-done.7.far_ref = bf16[384,1536]{1,0:T(8,128)(2,1)S(1)} collective-permute-done((bf16[384,1536]{1,0:T(8,128)(2,1)S(1)}, bf16[384,1536]{1,0:T(8,128)(2,1)S(1)}, u32[]{:S(2)}, u32[]{:S(2)}) %collective-permute-start.7) | collective-permute-done | bytes 1179680 | tf_op jit(solution)/shard_map/ppermute | solution.py:287
  106.6 1.8 %shard_map.118 = (f32[192,1536]{1,0:T(8,128)}, f32[192,1536]{1,0:T(8,128)}) custom-call(bf16[4,64,1536]{2,1,0:T(8,128)(2,1)S(1)} %all-to-all-done.1.x, bf16[4,128,192]{2,1,0:T(8,128)(2,1)S(1)} %get-tuple-element.24.hid_ref, bf16[4,128,192]{2,1,0:T(8,128)(2,1)S(1)} %get-tuple-element.25.back_ref, bf16[768,1536]{1,0:T(8,128)(2,1)S(1)} %collective-permute-done.6.came_ref, ...), custom_call_target="tpu_custom_call" | custom-call | flops 150994944 | bytes 4718592 | tf_op jit(solution)/shard_map/pallas_call | solution.py:289
  (2 shorter events, 0.0 us)
Async XLA Ops:
  0.6 5.5 %copy-start.1 = (bf16[128,64]{0,1:T(8,128)(2,1)S(1)}, bf16[128,64]{0,1:T(8,128)(2,1)}, u32[]{:S(2)}) copy-start(bf16[128,64]{0,1:T(8,128)(2,1)} %param.8) | copy-start | bytes 49156
  0.6 5.5 %copy-start.3 = (bf16[128,64]{0,1:T(8,128)(2,1)S(1)}, bf16[128,64]{0,1:T(8,128)(2,1)}, u32[]{:S(2)}) copy-start(bf16[128,64]{0,1:T(8,128)(2,1)} %param.9) | copy-start | bytes 49156
  0.7 5.5 %copy-start.5 = (s32[128,2]{0,1:T(2,128)S(1)}, s32[128,2]{0,1:T(2,128)}, u32[]{:S(2)}) copy-start(s32[128,2]{0,1:T(2,128)} %param.10) | copy-start | bytes 3076
  0.7 5.5 %copy-start.7 = (f32[128,2]{0,1:T(2,128)S(1)}, f32[128,2]{0,1:T(2,128)}, u32[]{:S(2)}) copy-start(f32[128,2]{0,1:T(2,128)} %param.11) | copy-start | bytes 3076
  0.7 29.5 %copy-start.9 = (f32[1536]{0:T(1024)S(1)}, f32[1536]{0:T(1024)}, u32[]{:S(2)}) copy-start(f32[1536]{0:T(1024)} %param.12) | copy-start | bytes 18436
  0.7 29.5 %copy-start.10 = (f32[1536]{0:T(1024)S(1)}, f32[1536]{0:T(1024)}, u32[]{:S(2)}) copy-start(f32[1536]{0:T(1024)} %param.13) | copy-start | bytes 18436
  2.1 50.2 %collective-permute-start = (bf16[384,1536]{1,0:T(8,128)(2,1)S(1)}, bf16[384,1536]{1,0:T(8,128)(2,1)S(1)}, u32[]{:S(2)}, u32[]{:S(2)}) collective-permute-start(bf16[384,1536]{1,0:T(8,128)(2,1)S(1)} %pad_maximum_fusion.w0), channel_id=1, source_target_pairs={{0,96},{96,0},{1,97},{97,1},{2,98},{98,2},{3,99},{99,3},{4,100},{1... | collective-permute-start | bytes 3538952 | tf_op jit(solution)/shard_map/ppermute | solution.py:244
  7.2 39.0 %all-to-all-start = ((bf16[48,16,128]{2,1,0:T(8,128)(2,1)}), bf16[48,16,128]{2,1,0:T(8,128)(2,1)S(1)}, u32[]{:S(2)}, u32[]{:S(2)}) async-start(bf16[48,16,128]{2,1,0:T(8,128)(2,1)} %bitcast.4), calls=%async_computation | async-start | bytes 393216 | tf_op jit(solution)/shard_map/all_to_all | solution.py:240
  28.2 25.9 %collective-permute-start.1 = (bf16[384,1536]{1,0:T(8,128)(2,1)S(1)}, bf16[384,1536]{1,0:T(8,128)(2,1)}, u32[]{:S(2)}, u32[]{:S(2)}) collective-permute-start(bf16[384,1536]{1,0:T(8,128)(2,1)S(1)} %pad_maximum_fusion.w0), channel_id=1, source_target_pairs={{0,24},{24,0},{1,25},{25,1},{2,26},{26,2},{3,27},{27,3},{4,28},{28... | collective-permute-start | bytes 3538952 | tf_op jit(solution)/shard_map/ppermute | solution.py:245
  46.5 0.9 copy-start
  47.4 12.9 %all-to-all-start.1 = ((bf16[4,64,1536]{2,1,0:T(8,128)(2,1)}), bf16[4,64,1536]{2,1,0:T(8,128)(2,1)S(1)}, u32[]{:S(2)}, u32[]{:S(2)}) async-start(bf16[4,64,1536]{2,1,0:T(8,128)(2,1)} %copy-done), calls=%async_computation.1 | async-start | bytes 1572864 | tf_op jit(solution)/shard_map/all_to_all | solution.py:254
  52.3 8.0 %collective-permute-start.2 = (bf16[384,1536]{1,0:T(8,128)(2,1)S(1)}, bf16[384,1536]{1,0:T(8,128)(2,1)}, u32[]{:S(2)}, u32[]{:S(2)}) collective-permute-start(bf16[384,1536]{1,0:T(8,128)(2,1)S(1)} %collective-permute-done.w1), channel_id=1, source_target_pairs={{0,24},{24,0},{1,25},{25,1},{2,26},{26,2},{3,27},{27,3},{4,28},{28... | collective-permute-start | bytes 3538952 | tf_op jit(solution)/shard_map/ppermute | solution.py:247
  64.0 11.2 %collective-permute-start.6 = (bf16[768,1536]{1,0:T(8,128)(2,1)S(1)}, bf16[768,1536]{1,0:T(8,128)(2,1)S(1)}, u32[]{:S(2)}, u32[]{:S(2)}) collective-permute-start(bf16[768,1536]{1,0:T(8,128)(2,1)S(1)} %shard_map.116), channel_id=1, source_target_pairs={{0,24},{24,0},{1,25},{25,1},{2,26},{26,2},{3,27},{27,3},{4,28},{28... | collective-permute-start | bytes 7077896 | tf_op jit(solution)/shard_map/ppermute | solution.py:279
  65.9 11.7 %collective-permute-start.3 = (bf16[32,3072]{1,0:T(8,128)(2,1)S(1)}, bf16[32,3072]{1,0:T(8,128)(2,1)S(1)}, u32[]{:S(2)}, u32[]{:S(2)}) collective-permute-start(bf16[32,3072]{1,0:T(8,128)(2,1)S(1)} %get-tuple-element.18), channel_id=1, source_target_pairs={{0,240},{48,192},{192,48},{240,0},{1,241},{49,193},{193,49},{241,1... | collective-permute-start | bytes 589832 | tf_op jit(solution)/shard_map/ppermute | solution.py:269
  69.2 11.1 %collective-permute-start.4 = (bf16[32,3072]{1,0:T(8,128)(2,1)S(1)}, bf16[32,3072]{1,0:T(8,128)(2,1)S(1)}, u32[]{:S(2)}, u32[]{:S(2)}) collective-permute-start(bf16[32,3072]{1,0:T(8,128)(2,1)S(1)} %get-tuple-element.19), channel_id=1, source_target_pairs={{0,48},{48,0},{1,49},{49,1},{2,50},{50,2},{3,51},{51,3},{4,52},{52... | collective-permute-start | bytes 589832 | tf_op jit(solution)/shard_map/ppermute | solution.py:269
  71.8 8.6 %collective-permute-start.5 = (bf16[32,3072]{1,0:T(8,128)(2,1)S(1)}, bf16[32,3072]{1,0:T(8,128)(2,1)S(1)}, u32[]{:S(2)}, u32[]{:S(2)}) collective-permute-start(bf16[32,3072]{1,0:T(8,128)(2,1)S(1)} %get-tuple-element.20), channel_id=1, source_target_pairs={{0,192},{192,0},{1,193},{193,1},{2,194},{194,2},{3,195},{195,3},{4... | collective-permute-start | bytes 589832 | tf_op jit(solution)/shard_map/ppermute | solution.py:269
  75.7 30.9 %collective-permute-start.7 = (bf16[384,1536]{1,0:T(8,128)(2,1)S(1)}, bf16[384,1536]{1,0:T(8,128)(2,1)S(1)}, u32[]{:S(2)}, u32[]{:S(2)}) collective-permute-start(bf16[384,1536]{1,0:T(8,128)(2,1)S(1)} %shard_map.117), channel_id=1, source_target_pairs={{0,96},{96,0},{1,97},{97,1},{2,98},{98,2},{3,99},{99,3},{4,100},{1... | collective-permute-start | bytes 3538952 | tf_op jit(solution)/shard_map/ppermute | solution.py:287
  80.4 24.1 %copy-start.2 = (bf16[128,64]{0,1:T(8,128)(2,1)S(1)}, bf16[128,64]{0,1:T(8,128)(2,1)}, u32[]{:S(2)}) copy-start(bf16[128,64]{0,1:T(8,128)(2,1)} %param.8) | copy-start | bytes 49156
  80.4 24.1 %copy-start.4 = (bf16[128,64]{0,1:T(8,128)(2,1)S(1)}, bf16[128,64]{0,1:T(8,128)(2,1)}, u32[]{:S(2)}) copy-start(bf16[128,64]{0,1:T(8,128)(2,1)} %param.9) | copy-start | bytes 49156
  80.4 24.1 %copy-start.6 = (s32[128,2]{0,1:T(2,128)S(1)}, s32[128,2]{0,1:T(2,128)}, u32[]{:S(2)}) copy-start(s32[128,2]{0,1:T(2,128)} %param.10) | copy-start | bytes 3076
  80.4 24.1 %copy-start.8 = (f32[128,2]{0,1:T(2,128)S(1)}, f32[128,2]{0,1:T(2,128)}, u32[]{:S(2)}) copy-start(f32[128,2]{0,1:T(2,128)} %param.11) | copy-start | bytes 3076
